TPU v7x, 128 devices: a whole 4x4x4 slice. The times are simulated.
128 devices in a mesh: wave: 4 (over z), tile: 32 (over y, x, core).
Axes of the slice: x: 4, y: 4, z: 4, core: 2. Of those that a mesh axis runs over, the one named last changes fastest.
Arguments:
- initial_fields: bfloat16 [16, 8, 1024, 1024], P('wave', None, 'tile'), may hold values from -6 to 6
- conductivity: float32 [1024, 1024], P('tile'), may hold values from 0.1 to 10
- wavenumbers: float32 [16], replicated, may hold values from 0.05 to 1.5
- quad_weights: float32 [16], replicated, may hold values from 0.05 to 0.3
- sweep_counts: int32 [16], replicated, may hold values from 1 to 8, as said below
- electrode_cells: int32 [64], replicated, may hold values from 0 to 1023
- source_pairs: int32 [8, 2], replicated, may hold values from 0 to 63, as said below
Outputs:
- potential: float32 [8, 1024, 1024], P('wave', 'tile')
Inputs may be any that keep to these rules, and one draw needn't show every extreme that they name: `sweep_counts`: each wavenumber gets at least one sweep and at most 8. `source_pairs`: the two electrodes of a source column are different electrodes.
All inputs are finite; a program needn't handle non-finite values.
Results may differ from a plain program's by a relative error of at most 0.0003.
Values may be sent and summed in bfloat16 or wider, within the bound.
A program may use at most 64 MiB of HBM per device.

v0:
```python
import jax
import jax.numpy as jnp
from jax import lax
from jax.sharding import PartitionSpec as P

ITERS = 8


LOWER = 0.1
UPPER = 2.0
THETA = (UPPER + LOWER) / 2.0
DELTA = (UPPER - LOWER) / 2.0
SIGMA_ONE = THETA / DELTA
CURRENT = 2.0


def with_halo(block, sides, width):
    for axis, dim in sides:
        count = lax.axis_size(axis)
        forward = [(i, i + 1) for i in range(count - 1)]
        backward = [(target, source) for source, target in forward]
        low = lax.ppermute(
            lax.slice_in_dim(block, block.shape[dim] - width, None, axis=dim), axis, forward
        )
        high = lax.ppermute(lax.slice_in_dim(block, 0, width, axis=dim), axis, backward)
        block = jnp.concatenate([low, block, high], axis=dim)
    return block


def neighbours(padded_rows, facets):
    face_north, face_south, face_west, face_east = facets
    centre = padded_rows[:, 1:-1]
    columns = jnp.pad(centre, ((0, 0), (0, 0), (1, 1)))
    total = face_north * padded_rows[:, :-2] + face_south * padded_rows[:, 2:]
    return total + face_west * columns[:, :, :-2] + face_east * columns[:, :, 2:]


def chebyshev_step(step, field, direction, rho_prev, residual, diag_k, active):
    scaled = residual / diag_k
    rho_next = 1.0 / (2.0 * SIGMA_ONE - rho_prev)
    first = step == 0
    keep = jnp.where(first, 0.0, rho_next * rho_prev)
    gain = jnp.where(first, 1.0 / THETA, 2.0 * rho_next / DELTA)
    moved = keep * direction + gain * scaled
    new_rho = jnp.where(first, 1.0 / SIGMA_ONE, rho_next)
    return (
        jnp.where(active, field + moved, field),
        jnp.where(active, moved, direction),
        jnp.where(active, new_rho, rho_prev),
    )


def local(
    initial_fields,
    conductivity,
    wavenumbers,
    quad_weights,
    sweep_counts,
    electrode_cells,
    source_pairs,
):
    row_count, col_count = conductivity.shape
    tile_pos = lax.axis_index("tile")
    wave_pos = lax.axis_index("wave")
    padded_cond = with_halo(conductivity, (("tile", 0),), 1)
    padded_full = jnp.pad(padded_cond, ((0, 0), (1, 1)))
    face_north = 0.5 * (conductivity + padded_full[:-2, 1:-1])
    face_south = 0.5 * (conductivity + padded_full[2:, 1:-1])
    face_west = 0.5 * (conductivity + padded_full[1:-1, :-2])
    face_east = 0.5 * (conductivity + padded_full[1:-1, 2:])
    facets = (face_north, face_south, face_west, face_east)
    diagonal = face_north + face_south + face_west + face_east
    per_group = initial_fields.shape[0]
    wave_values = lax.dynamic_slice_in_dim(wavenumbers, wave_pos * per_group, per_group)
    weights = lax.dynamic_slice_in_dim(quad_weights, wave_pos * per_group, per_group)
    counts = lax.dynamic_slice_in_dim(sweep_counts, wave_pos * per_group, per_group)
    source_count = initial_fields.shape[1]
    matches = (
        source_pairs[:, :, None]
        == jnp.arange(electrode_cells.shape[0], dtype=jnp.int32)[None, None, :]
    )
    electrode_rows = jnp.sum(jnp.where(matches, electrode_cells[None, None, :], 0), axis=2)
    column_one = (jnp.arange(col_count, dtype=jnp.int32) == 0).astype(jnp.float32)
    row_ids = tile_pos * row_count + jnp.arange(row_count, dtype=jnp.int32)
    positive = (row_ids[None, :] == electrode_rows[:, 0:1]).astype(jnp.float32)
    negative = (row_ids[None, :] == electrode_rows[:, 1:2]).astype(jnp.float32)
    sources = CURRENT * (positive - negative)[:, :, None] * column_one[None, None, :]

    def advance(start, repeats, squares, active, limit):
        source_terms = jnp.tile(sources, (repeats, 1, 1))
        diag_k = diagonal[None] + squares * conductivity[None]

        def sweep(step, carry):
            field_now, dir_now, rho_now = carry
            padded = with_halo(field_now, (("tile", 1),), 1)
            residual = source_terms - (diag_k * field_now - neighbours(padded, facets))
            live = jnp.logical_and(active(step), step < limit)
            return chebyshev_step(step, field_now, dir_now, rho_now, residual, diag_k, live)

        rho_start = jnp.full((start.shape[0], 1, 1), 1.0 / SIGMA_ONE, jnp.float32)
        return lax.fori_loop(0, ITERS, sweep, (start, jnp.zeros_like(start), rho_start))[0]

    def per_wave(total, item):
        field_start, wavenumber, weight, count = item
        solved = advance(
            field_start.astype(jnp.float32),
            1,
            wavenumber * wavenumber,
            lambda step: jnp.bool_(True),
            count,
        )
        return (total + weight * solved, None)

    summed, _ = lax.scan(
        per_wave,
        jnp.zeros((source_count, row_count, col_count), jnp.float32),
        (initial_fields, wave_values, weights, counts),
    )
    return lax.psum_scatter(summed, "wave", scatter_dimension=0, tiled=True)


def solution(mesh):
    placed = (P("wave", None, "tile", None), P("tile", None), P(), P(), P(), P(), P())
    return jax.shard_map(
        local, mesh=mesh, in_specs=placed, out_specs=P("wave", "tile", None), check_vma=False
    )
```

profile of v0, /device:TPU:0, one launch (start us, length us, event | category | flops | bytes accessed | tf_op | source)
XLA Modules:
  0.0 503.0 jit_solution(8654310361218106086)
XLA Ops:
  17.1 425.6 %while.42 = (s32[]{:T(128)}, f32[8,32,1024]{2,1,0:T(8,128)}, f32[4]{0:T(128)}, bf16[4,8,32,1024]{3,2,1,0:T(8,128)(2,1)}, f32[4]{0:T(128)}, /*index=5*/f32[32,102...) while((s32[]{:T(128)}, f32[8,32,1024]{2,1,0:T(8,128)}, ...), condition=%wide.region_4.5_spmd.clone, body=%wide.region_1.4_spmd.clone.sunk | while | flops 6619224 | bytes 15710408 | solution.py:114
  22.8 85.7 %while.43 = (s32[]{:T(128)}, f32[8,32,1024]{2,1,0:T(8,128)S(1)}, f32[8,32,1024]{2,1,0:T(8,128)S(1)}, f32[8,1,1]{0,2,1:T(1,128)S(1)}, s32[]{:T(128)}, /*index=5*/...) while((s32[]{:T(128)}, f32[8,32,1024]{2,1,0:T(8,128)S(1)}, ...), condition=%wide.region_3.3_spmd.clone, body=%wide.region_2.2_spmd.clone.sunk | while | flops 5242964 | bytes 9503301 | solution.py:101
  24.8 6.1 %collective-permute-start.1 = (f32[8,1,1024]{2,1,0:T(1,128)}, f32[8,1,1024]{2,1,0:T(1,128)}, u32[]{:S(2)}, u32[]{:S(2)}) collective-permute-start(f32[8,1,1024]{2,1,0:T(1,128)} %get-tuple-element.818), channel_id=1, source_target_pairs={{0,1},{1,2},{2,3},{3,4},{4,5},{5,6},{6,7},{7,8},{8,9},{9,10},{10,1... | collective-permute-start | bytes 98312 | tf_op jit(solution)/shard_map/while/body/eval_jaxpr/while/body/eval_jaxpr/ppermute | solution.py:22
  31.6 2.1 select_select_fusion.2
  36.1 4.8 collective-permute-start.1
  41.7 2.1 select_select_fusion.2
  46.2 5.4 %collective-permute-start.1 = (f32[8,1,1024]{2,1,0:T(1,128)}, f32[8,1,1024]{2,1,0:T(1,128)}, u32[]{:S(2)}, u32[]{:S(2)}) collective-permute-start(f32[8,1,1024]{2,1,0:T(1,128)} %get-tuple-element.818), channel_id=1, source_target_pairs={{0,1},{1,2},{2,3},{3,4},{4,5},{5,6},{6,7},{7,8},{8,9},{9,10},{10,1... | collective-permute-start | bytes 98312 | tf_op jit(solution)/shard_map/while/body/eval_jaxpr/while/body/eval_jaxpr/ppermute | solution.py:22
  52.4 2.1 select_select_fusion.2
  56.9 5.4 %collective-permute-start.1 = (f32[8,1,1024]{2,1,0:T(1,128)}, f32[8,1,1024]{2,1,0:T(1,128)}, u32[]{:S(2)}, u32[]{:S(2)}) collective-permute-start(f32[8,1,1024]{2,1,0:T(1,128)} %get-tuple-element.818), channel_id=1, source_target_pairs={{0,1},{1,2},{2,3},{3,4},{4,5},{5,6},{6,7},{7,8},{8,9},{9,10},{10,1... | collective-permute-start | bytes 98312 | tf_op jit(solution)/shard_map/while/body/eval_jaxpr/while/body/eval_jaxpr/ppermute | solution.py:22
  63.1 2.1 select_select_fusion.2
  67.6 5.4 %collective-permute-start.1 = (f32[8,1,1024]{2,1,0:T(1,128)}, f32[8,1,1024]{2,1,0:T(1,128)}, u32[]{:S(2)}, u32[]{:S(2)}) collective-permute-start(f32[8,1,1024]{2,1,0:T(1,128)} %get-tuple-element.818), channel_id=1, source_target_pairs={{0,1},{1,2},{2,3},{3,4},{4,5},{5,6},{6,7},{7,8},{8,9},{9,10},{10,1... | collective-permute-start | bytes 98312 | tf_op jit(solution)/shard_map/while/body/eval_jaxpr/while/body/eval_jaxpr/ppermute | solution.py:22
  73.8 2.1 select_select_fusion.2
  78.3 5.4 %collective-permute-start.1 = (f32[8,1,1024]{2,1,0:T(1,128)}, f32[8,1,1024]{2,1,0:T(1,128)}, u32[]{:S(2)}, u32[]{:S(2)}) collective-permute-start(f32[8,1,1024]{2,1,0:T(1,128)} %get-tuple-element.818), channel_id=1, source_target_pairs={{0,1},{1,2},{2,3},{3,4},{4,5},{5,6},{6,7},{7,8},{8,9},{9,10},{10,1... | collective-permute-start | bytes 98312 | tf_op jit(solution)/shard_map/while/body/eval_jaxpr/while/body/eval_jaxpr/ppermute | solution.py:22
  84.5 2.1 select_select_fusion.2
  89.0 5.4 %collective-permute-start.1 = (f32[8,1,1024]{2,1,0:T(1,128)}, f32[8,1,1024]{2,1,0:T(1,128)}, u32[]{:S(2)}, u32[]{:S(2)}) collective-permute-start(f32[8,1,1024]{2,1,0:T(1,128)} %get-tuple-element.818), channel_id=1, source_target_pairs={{0,1},{1,2},{2,3},{3,4},{4,5},{5,6},{6,7},{7,8},{8,9},{9,10},{10,1... | collective-permute-start | bytes 98312 | tf_op jit(solution)/shard_map/while/body/eval_jaxpr/while/body/eval_jaxpr/ppermute | solution.py:22
  95.2 2.1 select_select_fusion.2
  99.7 5.4 %collective-permute-start.1 = (f32[8,1,1024]{2,1,0:T(1,128)}, f32[8,1,1024]{2,1,0:T(1,128)}, u32[]{:S(2)}, u32[]{:S(2)}) collective-permute-start(f32[8,1,1024]{2,1,0:T(1,128)} %get-tuple-element.818), channel_id=1, source_target_pairs={{0,1},{1,2},{2,3},{3,4},{4,5},{5,6},{6,7},{7,8},{8,9},{9,10},{10,1... | collective-permute-start | bytes 98312 | tf_op jit(solution)/shard_map/while/body/eval_jaxpr/while/body/eval_jaxpr/ppermute | solution.py:22
  105.9 2.1 select_select_fusion.2
  117.4 95.7 %while.43 = (s32[]{:T(128)}, f32[8,32,1024]{2,1,0:T(8,128)S(1)}, f32[8,32,1024]{2,1,0:T(8,128)S(1)}, f32[8,1,1]{0,2,1:T(1,128)S(1)}, s32[]{:T(128)}, /*index=5*/...) while((s32[]{:T(128)}, f32[8,32,1024]{2,1,0:T(8,128)S(1)}, ...), condition=%wide.region_3.3_spmd.clone, body=%wide.region_2.2_spmd.clone.sunk | while | flops 5242964 | bytes 9503301 | solution.py:101
  119.4 5.4 %collective-permute-start.1 = (f32[8,1,1024]{2,1,0:T(1,128)}, f32[8,1,1024]{2,1,0:T(1,128)}, u32[]{:S(2)}, u32[]{:S(2)}) collective-permute-start(f32[8,1,1024]{2,1,0:T(1,128)} %get-tuple-element.818), channel_id=1, source_target_pairs={{0,1},{1,2},{2,3},{3,4},{4,5},{5,6},{6,7},{7,8},{8,9},{9,10},{10,1... | collective-permute-start | bytes 98312 | tf_op jit(solution)/shard_map/while/body/eval_jaxpr/while/body/eval_jaxpr/ppermute | solution.py:22
  125.5 2.1 select_select_fusion.2
  130.1 5.4 %collective-permute-start.1 = (f32[8,1,1024]{2,1,0:T(1,128)}, f32[8,1,1024]{2,1,0:T(1,128)}, u32[]{:S(2)}, u32[]{:S(2)}) collective-permute-start(f32[8,1,1024]{2,1,0:T(1,128)} %get-tuple-element.818), channel_id=1, source_target_pairs={{0,1},{1,2},{2,3},{3,4},{4,5},{5,6},{6,7},{7,8},{8,9},{9,10},{10,1... | collective-permute-start | bytes 98312 | tf_op jit(solution)/shard_map/while/body/eval_jaxpr/while/body/eval_jaxpr/ppermute | solution.py:22
  136.2 2.1 select_select_fusion.2
  140.8 5.4 %collective-permute-start.1 = (f32[8,1,1024]{2,1,0:T(1,128)}, f32[8,1,1024]{2,1,0:T(1,128)}, u32[]{:S(2)}, u32[]{:S(2)}) collective-permute-start(f32[8,1,1024]{2,1,0:T(1,128)} %get-tuple-element.818), channel_id=1, source_target_pairs={{0,1},{1,2},{2,3},{3,4},{4,5},{5,6},{6,7},{7,8},{8,9},{9,10},{10,1... | collective-permute-start | bytes 98312 | tf_op jit(solution)/shard_map/while/body/eval_jaxpr/while/body/eval_jaxpr/ppermute | solution.py:22
  146.9 2.1 select_select_fusion.2
  151.5 7.1 %collective-permute-start.1 = (f32[8,1,1024]{2,1,0:T(1,128)}, f32[8,1,1024]{2,1,0:T(1,128)}, u32[]{:S(2)}, u32[]{:S(2)}) collective-permute-start(f32[8,1,1024]{2,1,0:T(1,128)} %get-tuple-element.818), channel_id=1, source_target_pairs={{0,1},{1,2},{2,3},{3,4},{4,5},{5,6},{6,7},{7,8},{8,9},{9,10},{10,1... | collective-permute-start | bytes 98312 | tf_op jit(solution)/shard_map/while/body/eval_jaxpr/while/body/eval_jaxpr/ppermute | solution.py:22
  159.3 2.1 select_select_fusion.2
  163.8 7.5 %collective-permute-start.1 = (f32[8,1,1024]{2,1,0:T(1,128)}, f32[8,1,1024]{2,1,0:T(1,128)}, u32[]{:S(2)}, u32[]{:S(2)}) collective-permute-start(f32[8,1,1024]{2,1,0:T(1,128)} %get-tuple-element.818), channel_id=1, source_target_pairs={{0,1},{1,2},{2,3},{3,4},{4,5},{5,6},{6,7},{7,8},{8,9},{9,10},{10,1... | collective-permute-start | bytes 98312 | tf_op jit(solution)/shard_map/while/body/eval_jaxpr/while/body/eval_jaxpr/ppermute | solution.py:22
  172.1 2.1 select_select_fusion.2
  176.6 7.5 %collective-permute-start.1 = (f32[8,1,1024]{2,1,0:T(1,128)}, f32[8,1,1024]{2,1,0:T(1,128)}, u32[]{:S(2)}, u32[]{:S(2)}) collective-permute-start(f32[8,1,1024]{2,1,0:T(1,128)} %get-tuple-element.818), channel_id=1, source_target_pairs={{0,1},{1,2},{2,3},{3,4},{4,5},{5,6},{6,7},{7,8},{8,9},{9,10},{10,1... | collective-permute-start | bytes 98312 | tf_op jit(solution)/shard_map/while/body/eval_jaxpr/while/body/eval_jaxpr/ppermute | solution.py:22
  184.9 2.1 select_select_fusion.2
  189.4 7.5 %collective-permute-start.1 = (f32[8,1,1024]{2,1,0:T(1,128)}, f32[8,1,1024]{2,1,0:T(1,128)}, u32[]{:S(2)}, u32[]{:S(2)}) collective-permute-start(f32[8,1,1024]{2,1,0:T(1,128)} %get-tuple-element.818), channel_id=1, source_target_pairs={{0,1},{1,2},{2,3},{3,4},{4,5},{5,6},{6,7},{7,8},{8,9},{9,10},{10,1... | collective-permute-start | bytes 98312 | tf_op jit(solution)/shard_map/while/body/eval_jaxpr/while/body/eval_jaxpr/ppermute | solution.py:22
  197.7 2.1 select_select_fusion.2
  202.2 7.5 %collective-permute-start.1 = (f32[8,1,1024]{2,1,0:T(1,128)}, f32[8,1,1024]{2,1,0:T(1,128)}, u32[]{:S(2)}, u32[]{:S(2)}) collective-permute-start(f32[8,1,1024]{2,1,0:T(1,128)} %get-tuple-element.818), channel_id=1, source_target_pairs={{0,1},{1,2},{2,3},{3,4},{4,5},{5,6},{6,7},{7,8},{8,9},{9,10},{10,1... | collective-permute-start | bytes 98312 | tf_op jit(solution)/shard_map/while/body/eval_jaxpr/while/body/eval_jaxpr/ppermute | solution.py:22
  210.5 2.1 select_select_fusion.2
  214.3 3.1 select_add_fusion.2
  223.2 102.5 %while.43 = (s32[]{:T(128)}, f32[8,32,1024]{2,1,0:T(8,128)S(1)}, f32[8,32,1024]{2,1,0:T(8,128)S(1)}, f32[8,1,1]{0,2,1:T(1,128)S(1)}, s32[]{:T(128)}, /*index=5*/...) while((s32[]{:T(128)}, f32[8,32,1024]{2,1,0:T(8,128)S(1)}, ...), condition=%wide.region_3.3_spmd.clone, body=%wide.region_2.2_spmd.clone.sunk | while | flops 5242964 | bytes 9503301 | solution.py:101
  225.2 7.5 %collective-permute-start.1 = (f32[8,1,1024]{2,1,0:T(1,128)}, f32[8,1,1024]{2,1,0:T(1,128)}, u32[]{:S(2)}, u32[]{:S(2)}) collective-permute-start(f32[8,1,1024]{2,1,0:T(1,128)} %get-tuple-element.818), channel_id=1, source_target_pairs={{0,1},{1,2},{2,3},{3,4},{4,5},{5,6},{6,7},{7,8},{8,9},{9,10},{10,1... | collective-permute-start | bytes 98312 | tf_op jit(solution)/shard_map/while/body/eval_jaxpr/while/body/eval_jaxpr/ppermute | solution.py:22
  233.5 2.1 select_select_fusion.2
  238.0 7.5 %collective-permute-start.1 = (f32[8,1,1024]{2,1,0:T(1,128)}, f32[8,1,1024]{2,1,0:T(1,128)}, u32[]{:S(2)}, u32[]{:S(2)}) collective-permute-start(f32[8,1,1024]{2,1,0:T(1,128)} %get-tuple-element.818), channel_id=1, source_target_pairs={{0,1},{1,2},{2,3},{3,4},{4,5},{5,6},{6,7},{7,8},{8,9},{9,10},{10,1... | collective-permute-start | bytes 98312 | tf_op jit(solution)/shard_map/while/body/eval_jaxpr/while/body/eval_jaxpr/ppermute | solution.py:22
  246.3 2.1 select_select_fusion.2
  250.8 7.5 %collective-permute-start.1 = (f32[8,1,1024]{2,1,0:T(1,128)}, f32[8,1,1024]{2,1,0:T(1,128)}, u32[]{:S(2)}, u32[]{:S(2)}) collective-permute-start(f32[8,1,1024]{2,1,0:T(1,128)} %get-tuple-element.818), channel_id=1, source_target_pairs={{0,1},{1,2},{2,3},{3,4},{4,5},{5,6},{6,7},{7,8},{8,9},{9,10},{10,1... | collective-permute-start | bytes 98312 | tf_op jit(solution)/shard_map/while/body/eval_jaxpr/while/body/eval_jaxpr/ppermute | solution.py:22
  259.1 2.1 select_select_fusion.2
  263.6 7.5 %collective-permute-start.1 = (f32[8,1,1024]{2,1,0:T(1,128)}, f32[8,1,1024]{2,1,0:T(1,128)}, u32[]{:S(2)}, u32[]{:S(2)}) collective-permute-start(f32[8,1,1024]{2,1,0:T(1,128)} %get-tuple-element.818), channel_id=1, source_target_pairs={{0,1},{1,2},{2,3},{3,4},{4,5},{5,6},{6,7},{7,8},{8,9},{9,10},{10,1... | collective-permute-start | bytes 98312 | tf_op jit(solution)/shard_map/while/body/eval_jaxpr/while/body/eval_jaxpr/ppermute | solution.py:22
  271.9 2.1 select_select_fusion.2
  276.4 7.5 %collective-permute-start.1 = (f32[8,1,1024]{2,1,0:T(1,128)}, f32[8,1,1024]{2,1,0:T(1,128)}, u32[]{:S(2)}, u32[]{:S(2)}) collective-permute-start(f32[8,1,1024]{2,1,0:T(1,128)} %get-tuple-element.818), channel_id=1, source_target_pairs={{0,1},{1,2},{2,3},{3,4},{4,5},{5,6},{6,7},{7,8},{8,9},{9,10},{10,1... | collective-permute-start | bytes 98312 | tf_op jit(solution)/shard_map/while/body/eval_jaxpr/while/body/eval_jaxpr/ppermute | solution.py:22
  284.7 2.1 select_select_fusion.2
  289.2 7.5 %collective-permute-start.1 = (f32[8,1,1024]{2,1,0:T(1,128)}, f32[8,1,1024]{2,1,0:T(1,128)}, u32[]{:S(2)}, u32[]{:S(2)}) collective-permute-start(f32[8,1,1024]{2,1,0:T(1,128)} %get-tuple-element.818), channel_id=1, source_target_pairs={{0,1},{1,2},{2,3},{3,4},{4,5},{5,6},{6,7},{7,8},{8,9},{9,10},{10,1... | collective-permute-start | bytes 98312 | tf_op jit(solution)/shard_map/while/body/eval_jaxpr/while/body/eval_jaxpr/ppermute | solution.py:22
  302.0 7.5 %collective-permute-start.1 = (f32[8,1,1024]{2,1,0:T(1,128)}, f32[8,1,1024]{2,1,0:T(1,128)}, u32[]{:S(2)}, u32[]{:S(2)}) collective-permute-start(f32[8,1,1024]{2,1,0:T(1,128)} %get-tuple-element.818), channel_id=1, source_target_pairs={{0,1},{1,2},{2,3},{3,4},{4,5},{5,6},{6,7},{7,8},{8,9},{9,10},{10,1... | collective-permute-start | bytes 98312 | tf_op jit(solution)/shard_map/while/body/eval_jaxpr/while/body/eval_jaxpr/ppermute | solution.py:22
  310.3 2.1 select_select_fusion.2
  314.8 7.5 %collective-permute-start.1 = (f32[8,1,1024]{2,1,0:T(1,128)}, f32[8,1,1024]{2,1,0:T(1,128)}, u32[]{:S(2)}, u32[]{:S(2)}) collective-permute-start(f32[8,1,1024]{2,1,0:T(1,128)} %get-tuple-element.818), channel_id=1, source_target_pairs={{0,1},{1,2},{2,3},{3,4},{4,5},{5,6},{6,7},{7,8},{8,9},{9,10},{10,1... | collective-permute-start | bytes 98312 | tf_op jit(solution)/shard_map/while/body/eval_jaxpr/while/body/eval_jaxpr/ppermute | solution.py:22
  327.0 3.1 select_add_fusion.2
  335.8 102.5 %while.43 = (s32[]{:T(128)}, f32[8,32,1024]{2,1,0:T(8,128)S(1)}, f32[8,32,1024]{2,1,0:T(8,128)S(1)}, f32[8,1,1]{0,2,1:T(1,128)S(1)}, s32[]{:T(128)}, /*index=5*/...) while((s32[]{:T(128)}, f32[8,32,1024]{2,1,0:T(8,128)S(1)}, ...), condition=%wide.region_3.3_spmd.clone, body=%wide.region_2.2_spmd.clone.sunk | while | flops 5242964 | bytes 9503301 | solution.py:101
  337.8 7.5 %collective-permute-start.1 = (f32[8,1,1024]{2,1,0:T(1,128)}, f32[8,1,1024]{2,1,0:T(1,128)}, u32[]{:S(2)}, u32[]{:S(2)}) collective-permute-start(f32[8,1,1024]{2,1,0:T(1,128)} %get-tuple-element.818), channel_id=1, source_target_pairs={{0,1},{1,2},{2,3},{3,4},{4,5},{5,6},{6,7},{7,8},{8,9},{9,10},{10,1... | collective-permute-start | bytes 98312 | tf_op jit(solution)/shard_map/while/body/eval_jaxpr/while/body/eval_jaxpr/ppermute | solution.py:22
  350.6 7.5 %collective-permute-start.1 = (f32[8,1,1024]{2,1,0:T(1,128)}, f32[8,1,1024]{2,1,0:T(1,128)}, u32[]{:S(2)}, u32[]{:S(2)}) collective-permute-start(f32[8,1,1024]{2,1,0:T(1,128)} %get-tuple-element.818), channel_id=1, source_target_pairs={{0,1},{1,2},{2,3},{3,4},{4,5},{5,6},{6,7},{7,8},{8,9},{9,10},{10,1... | collective-permute-start | bytes 98312 | tf_op jit(solution)/shard_map/while/body/eval_jaxpr/while/body/eval_jaxpr/ppermute | solution.py:22
  363.4 7.5 %collective-permute-start.1 = (f32[8,1,1024]{2,1,0:T(1,128)}, f32[8,1,1024]{2,1,0:T(1,128)}, u32[]{:S(2)}, u32[]{:S(2)}) collective-permute-start(f32[8,1,1024]{2,1,0:T(1,128)} %get-tuple-element.818), channel_id=1, source_target_pairs={{0,1},{1,2},{2,3},{3,4},{4,5},{5,6},{6,7},{7,8},{8,9},{9,10},{10,1... | collective-permute-start | bytes 98312 | tf_op jit(solution)/shard_map/while/body/eval_jaxpr/while/body/eval_jaxpr/ppermute | solution.py:22
  376.2 7.5 %collective-permute-start.1 = (f32[8,1,1024]{2,1,0:T(1,128)}, f32[8,1,1024]{2,1,0:T(1,128)}, u32[]{:S(2)}, u32[]{:S(2)}) collective-permute-start(f32[8,1,1024]{2,1,0:T(1,128)} %get-tuple-element.818), channel_id=1, source_target_pairs={{0,1},{1,2},{2,3},{3,4},{4,5},{5,6},{6,7},{7,8},{8,9},{9,10},{10,1... | collective-permute-start | bytes 98312 | tf_op jit(solution)/shard_map/while/body/eval_jaxpr/while/body/eval_jaxpr/ppermute | solution.py:22
  389.0 7.5 %collective-permute-start.1 = (f32[8,1,1024]{2,1,0:T(1,128)}, f32[8,1,1024]{2,1,0:T(1,128)}, u32[]{:S(2)}, u32[]{:S(2)}) collective-permute-start(f32[8,1,1024]{2,1,0:T(1,128)} %get-tuple-element.818), channel_id=1, source_target_pairs={{0,1},{1,2},{2,3},{3,4},{4,5},{5,6},{6,7},{7,8},{8,9},{9,10},{10,1... | collective-permute-start | bytes 98312 | tf_op jit(solution)/shard_map/while/body/eval_jaxpr/while/body/eval_jaxpr/ppermute | solution.py:22
  397.3 2.1 select_select_fusion.2
  401.8 7.5 %collective-permute-start.1 = (f32[8,1,1024]{2,1,0:T(1,128)}, f32[8,1,1024]{2,1,0:T(1,128)}, u32[]{:S(2)}, u32[]{:S(2)}) collective-permute-start(f32[8,1,1024]{2,1,0:T(1,128)} %get-tuple-element.818), channel_id=1, source_target_pairs={{0,1},{1,2},{2,3},{3,4},{4,5},{5,6},{6,7},{7,8},{8,9},{9,10},{10,1... | collective-permute-start | bytes 98312 | tf_op jit(solution)/shard_map/while/body/eval_jaxpr/while/body/eval_jaxpr/ppermute | solution.py:22
  414.6 7.5 %collective-permute-start.1 = (f32[8,1,1024]{2,1,0:T(1,128)}, f32[8,1,1024]{2,1,0:T(1,128)}, u32[]{:S(2)}, u32[]{:S(2)}) collective-permute-start(f32[8,1,1024]{2,1,0:T(1,128)} %get-tuple-element.818), channel_id=1, source_target_pairs={{0,1},{1,2},{2,3},{3,4},{4,5},{5,6},{6,7},{7,8},{8,9},{9,10},{10,1... | collective-permute-start | bytes 98312 | tf_op jit(solution)/shard_map/while/body/eval_jaxpr/while/body/eval_jaxpr/ppermute | solution.py:22
  427.4 7.5 %collective-permute-start.1 = (f32[8,1,1024]{2,1,0:T(1,128)}, f32[8,1,1024]{2,1,0:T(1,128)}, u32[]{:S(2)}, u32[]{:S(2)}) collective-permute-start(f32[8,1,1024]{2,1,0:T(1,128)} %get-tuple-element.818), channel_id=1, source_target_pairs={{0,1},{1,2},{2,3},{3,4},{4,5},{5,6},{6,7},{7,8},{8,9},{9,10},{10,1... | collective-permute-start | bytes 98312 | tf_op jit(solution)/shard_map/while/body/eval_jaxpr/while/body/eval_jaxpr/ppermute | solution.py:22
  439.6 3.1 select_add_fusion.2
  442.7 53.4 %reduce-scatter.2.cloned.1.call-done = f32[2,32,1024]{2,1,0:T(8,128)} async-done(((f32[8,32,1024]{2,1,0:T(8,128)}), f32[2,32,1024]{2,1,0:T(8,128)}) %reduce-scatter.2.cloned.1.call-update) | async-done | bytes 262160 | tf_op jit(solution)/shard_map/reduce_scatter | solution.py:119
  (364 shorter events, 130.9 us)
Async XLA Ops:
  6.5 489.6 %reduce-scatter.2.cloned.1.call-start = ((), (), s32[]{:S(2)}) async-start(), calls=%async_computation.1 | async-start | bytes 1310720 | tf_op jit(solution)/shard_map/reduce_scatter | solution.py:119
  7.3 6.8 %collective-permute-start.2 = (f32[1,1024]{1,0:T(1,128)S(1)}, f32[1,1024]{1,0:T(1,128)S(1)}, u32[]{:S(2)}, u32[]{:S(2)}) collective-permute-start(f32[1,1024]{1,0:T(1,128)S(1)} %get-tuple-element.628), channel_id=1, source_target_pairs={{0,1},{1,2},{2,3},{3,4},{4,5},{5,6},{6,7},{7,8},{8,9},{9,10},{10,1... | collective-permute-start | bytes 12296 | tf_op jit(solution)/shard_map/ppermute | solution.py:22
  23.5 8.1 %collective-permute-start = (f32[8,1,1024]{2,1,0:T(1,128)}, f32[8,1,1024]{2,1,0:T(1,128)}, u32[]{:S(2)}, u32[]{:S(2)}) collective-permute-start(f32[8,1,1024]{2,1,0:T(1,128)} %get-tuple-element.817), channel_id=1, source_target_pairs={{1,0},{2,1},{3,2},{4,3},{5,4},{6,5},{7,6},{8,7},{9,8},{10,9},{11,1... | collective-permute-start | bytes 98312 | tf_op jit(solution)/shard_map/while/body/eval_jaxpr/while/body/eval_jaxpr/ppermute | solution.py:25
  24.8 6.8 %collective-permute-start.1 = (f32[8,1,1024]{2,1,0:T(1,128)}, f32[8,1,1024]{2,1,0:T(1,128)}, u32[]{:S(2)}, u32[]{:S(2)}) collective-permute-start(f32[8,1,1024]{2,1,0:T(1,128)} %get-tuple-element.818), channel_id=1, source_target_pairs={{0,1},{1,2},{2,3},{3,4},{4,5},{5,6},{6,7},{7,8},{8,9},{9,10},{10,1... | collective-permute-start | bytes 98312 | tf_op jit(solution)/shard_map/while/body/eval_jaxpr/while/body/eval_jaxpr/ppermute | solution.py:22
  34.8 6.9 %collective-permute-start = (f32[8,1,1024]{2,1,0:T(1,128)}, f32[8,1,1024]{2,1,0:T(1,128)}, u32[]{:S(2)}, u32[]{:S(2)}) collective-permute-start(f32[8,1,1024]{2,1,0:T(1,128)} %get-tuple-element.817), channel_id=1, source_target_pairs={{1,0},{2,1},{3,2},{4,3},{5,4},{6,5},{7,6},{8,7},{9,8},{10,9},{11,1... | collective-permute-start | bytes 98312 | tf_op jit(solution)/shard_map/while/body/eval_jaxpr/while/body/eval_jaxpr/ppermute | solution.py:25
  45.0 7.4 %collective-permute-start = (f32[8,1,1024]{2,1,0:T(1,128)}, f32[8,1,1024]{2,1,0:T(1,128)}, u32[]{:S(2)}, u32[]{:S(2)}) collective-permute-start(f32[8,1,1024]{2,1,0:T(1,128)} %get-tuple-element.817), channel_id=1, source_target_pairs={{1,0},{2,1},{3,2},{4,3},{5,4},{6,5},{7,6},{8,7},{9,8},{10,9},{11,1... | collective-permute-start | bytes 98312 | tf_op jit(solution)/shard_map/while/body/eval_jaxpr/while/body/eval_jaxpr/ppermute | solution.py:25
  46.2 6.2 %collective-permute-start.1 = (f32[8,1,1024]{2,1,0:T(1,128)}, f32[8,1,1024]{2,1,0:T(1,128)}, u32[]{:S(2)}, u32[]{:S(2)}) collective-permute-start(f32[8,1,1024]{2,1,0:T(1,128)} %get-tuple-element.818), channel_id=1, source_target_pairs={{0,1},{1,2},{2,3},{3,4},{4,5},{5,6},{6,7},{7,8},{8,9},{9,10},{10,1... | collective-permute-start | bytes 98312 | tf_op jit(solution)/shard_map/while/body/eval_jaxpr/while/body/eval_jaxpr/ppermute | solution.py:22
  55.7 7.4 %collective-permute-start = (f32[8,1,1024]{2,1,0:T(1,128)}, f32[8,1,1024]{2,1,0:T(1,128)}, u32[]{:S(2)}, u32[]{:S(2)}) collective-permute-start(f32[8,1,1024]{2,1,0:T(1,128)} %get-tuple-element.817), channel_id=1, source_target_pairs={{1,0},{2,1},{3,2},{4,3},{5,4},{6,5},{7,6},{8,7},{9,8},{10,9},{11,1... | collective-permute-start | bytes 98312 | tf_op jit(solution)/shard_map/while/body/eval_jaxpr/while/body/eval_jaxpr/ppermute | solution.py:25
  56.9 6.2 %collective-permute-start.1 = (f32[8,1,1024]{2,1,0:T(1,128)}, f32[8,1,1024]{2,1,0:T(1,128)}, u32[]{:S(2)}, u32[]{:S(2)}) collective-permute-start(f32[8,1,1024]{2,1,0:T(1,128)} %get-tuple-element.818), channel_id=1, source_target_pairs={{0,1},{1,2},{2,3},{3,4},{4,5},{5,6},{6,7},{7,8},{8,9},{9,10},{10,1... | collective-permute-start | bytes 98312 | tf_op jit(solution)/shard_map/while/body/eval_jaxpr/while/body/eval_jaxpr/ppermute | solution.py:22
  66.4 7.4 %collective-permute-start = (f32[8,1,1024]{2,1,0:T(1,128)}, f32[8,1,1024]{2,1,0:T(1,128)}, u32[]{:S(2)}, u32[]{:S(2)}) collective-permute-start(f32[8,1,1024]{2,1,0:T(1,128)} %get-tuple-element.817), channel_id=1, source_target_pairs={{1,0},{2,1},{3,2},{4,3},{5,4},{6,5},{7,6},{8,7},{9,8},{10,9},{11,1... | collective-permute-start | bytes 98312 | tf_op jit(solution)/shard_map/while/body/eval_jaxpr/while/body/eval_jaxpr/ppermute | solution.py:25
  67.6 6.2 %collective-permute-start.1 = (f32[8,1,1024]{2,1,0:T(1,128)}, f32[8,1,1024]{2,1,0:T(1,128)}, u32[]{:S(2)}, u32[]{:S(2)}) collective-permute-start(f32[8,1,1024]{2,1,0:T(1,128)} %get-tuple-element.818), channel_id=1, source_target_pairs={{0,1},{1,2},{2,3},{3,4},{4,5},{5,6},{6,7},{7,8},{8,9},{9,10},{10,1... | collective-permute-start | bytes 98312 | tf_op jit(solution)/shard_map/while/body/eval_jaxpr/while/body/eval_jaxpr/ppermute | solution.py:22
  77.0 7.4 %collective-permute-start = (f32[8,1,1024]{2,1,0:T(1,128)}, f32[8,1,1024]{2,1,0:T(1,128)}, u32[]{:S(2)}, u32[]{:S(2)}) collective-permute-start(f32[8,1,1024]{2,1,0:T(1,128)} %get-tuple-element.817), channel_id=1, source_target_pairs={{1,0},{2,1},{3,2},{4,3},{5,4},{6,5},{7,6},{8,7},{9,8},{10,9},{11,1... | collective-permute-start | bytes 98312 | tf_op jit(solution)/shard_map/while/body/eval_jaxpr/while/body/eval_jaxpr/ppermute | solution.py:25
  78.3 6.2 %collective-permute-start.1 = (f32[8,1,1024]{2,1,0:T(1,128)}, f32[8,1,1024]{2,1,0:T(1,128)}, u32[]{:S(2)}, u32[]{:S(2)}) collective-permute-start(f32[8,1,1024]{2,1,0:T(1,128)} %get-tuple-element.818), channel_id=1, source_target_pairs={{0,1},{1,2},{2,3},{3,4},{4,5},{5,6},{6,7},{7,8},{8,9},{9,10},{10,1... | collective-permute-start | bytes 98312 | tf_op jit(solution)/shard_map/while/body/eval_jaxpr/while/body/eval_jaxpr/ppermute | solution.py:22
  87.7 7.4 %collective-permute-start = (f32[8,1,1024]{2,1,0:T(1,128)}, f32[8,1,1024]{2,1,0:T(1,128)}, u32[]{:S(2)}, u32[]{:S(2)}) collective-permute-start(f32[8,1,1024]{2,1,0:T(1,128)} %get-tuple-element.817), channel_id=1, source_target_pairs={{1,0},{2,1},{3,2},{4,3},{5,4},{6,5},{7,6},{8,7},{9,8},{10,9},{11,1... | collective-permute-start | bytes 98312 | tf_op jit(solution)/shard_map/while/body/eval_jaxpr/while/body/eval_jaxpr/ppermute | solution.py:25
  89.0 6.2 %collective-permute-start.1 = (f32[8,1,1024]{2,1,0:T(1,128)}, f32[8,1,1024]{2,1,0:T(1,128)}, u32[]{:S(2)}, u32[]{:S(2)}) collective-permute-start(f32[8,1,1024]{2,1,0:T(1,128)} %get-tuple-element.818), channel_id=1, source_target_pairs={{0,1},{1,2},{2,3},{3,4},{4,5},{5,6},{6,7},{7,8},{8,9},{9,10},{10,1... | collective-permute-start | bytes 98312 | tf_op jit(solution)/shard_map/while/body/eval_jaxpr/while/body/eval_jaxpr/ppermute | solution.py:22
  98.4 7.4 %collective-permute-start = (f32[8,1,1024]{2,1,0:T(1,128)}, f32[8,1,1024]{2,1,0:T(1,128)}, u32[]{:S(2)}, u32[]{:S(2)}) collective-permute-start(f32[8,1,1024]{2,1,0:T(1,128)} %get-tuple-element.817), channel_id=1, source_target_pairs={{1,0},{2,1},{3,2},{4,3},{5,4},{6,5},{7,6},{8,7},{9,8},{10,9},{11,1... | collective-permute-start | bytes 98312 | tf_op jit(solution)/shard_map/while/body/eval_jaxpr/while/body/eval_jaxpr/ppermute | solution.py:25
  99.7 6.2 %collective-permute-start.1 = (f32[8,1,1024]{2,1,0:T(1,128)}, f32[8,1,1024]{2,1,0:T(1,128)}, u32[]{:S(2)}, u32[]{:S(2)}) collective-permute-start(f32[8,1,1024]{2,1,0:T(1,128)} %get-tuple-element.818), channel_id=1, source_target_pairs={{0,1},{1,2},{2,3},{3,4},{4,5},{5,6},{6,7},{7,8},{8,9},{9,10},{10,1... | collective-permute-start | bytes 98312 | tf_op jit(solution)/shard_map/while/body/eval_jaxpr/while/body/eval_jaxpr/ppermute | solution.py:22
  118.1 7.4 %collective-permute-start = (f32[8,1,1024]{2,1,0:T(1,128)}, f32[8,1,1024]{2,1,0:T(1,128)}, u32[]{:S(2)}, u32[]{:S(2)}) collective-permute-start(f32[8,1,1024]{2,1,0:T(1,128)} %get-tuple-element.817), channel_id=1, source_target_pairs={{1,0},{2,1},{3,2},{4,3},{5,4},{6,5},{7,6},{8,7},{9,8},{10,9},{11,1... | collective-permute-start | bytes 98312 | tf_op jit(solution)/shard_map/while/body/eval_jaxpr/while/body/eval_jaxpr/ppermute | solution.py:25
  119.4 6.2 %collective-permute-start.1 = (f32[8,1,1024]{2,1,0:T(1,128)}, f32[8,1,1024]{2,1,0:T(1,128)}, u32[]{:S(2)}, u32[]{:S(2)}) collective-permute-start(f32[8,1,1024]{2,1,0:T(1,128)} %get-tuple-element.818), channel_id=1, source_target_pairs={{0,1},{1,2},{2,3},{3,4},{4,5},{5,6},{6,7},{7,8},{8,9},{9,10},{10,1... | collective-permute-start | bytes 98312 | tf_op jit(solution)/shard_map/while/body/eval_jaxpr/while/body/eval_jaxpr/ppermute | solution.py:22
  128.8 7.4 %collective-permute-start = (f32[8,1,1024]{2,1,0:T(1,128)}, f32[8,1,1024]{2,1,0:T(1,128)}, u32[]{:S(2)}, u32[]{:S(2)}) collective-permute-start(f32[8,1,1024]{2,1,0:T(1,128)} %get-tuple-element.817), channel_id=1, source_target_pairs={{1,0},{2,1},{3,2},{4,3},{5,4},{6,5},{7,6},{8,7},{9,8},{10,9},{11,1... | collective-permute-start | bytes 98312 | tf_op jit(solution)/shard_map/while/body/eval_jaxpr/while/body/eval_jaxpr/ppermute | solution.py:25
  130.1 6.2 %collective-permute-start.1 = (f32[8,1,1024]{2,1,0:T(1,128)}, f32[8,1,1024]{2,1,0:T(1,128)}, u32[]{:S(2)}, u32[]{:S(2)}) collective-permute-start(f32[8,1,1024]{2,1,0:T(1,128)} %get-tuple-element.818), channel_id=1, source_target_pairs={{0,1},{1,2},{2,3},{3,4},{4,5},{5,6},{6,7},{7,8},{8,9},{9,10},{10,1... | collective-permute-start | bytes 98312 | tf_op jit(solution)/shard_map/while/body/eval_jaxpr/while/body/eval_jaxpr/ppermute | solution.py:22
  139.5 7.4 %collective-permute-start = (f32[8,1,1024]{2,1,0:T(1,128)}, f32[8,1,1024]{2,1,0:T(1,128)}, u32[]{:S(2)}, u32[]{:S(2)}) collective-permute-start(f32[8,1,1024]{2,1,0:T(1,128)} %get-tuple-element.817), channel_id=1, source_target_pairs={{1,0},{2,1},{3,2},{4,3},{5,4},{6,5},{7,6},{8,7},{9,8},{10,9},{11,1... | collective-permute-start | bytes 98312 | tf_op jit(solution)/shard_map/while/body/eval_jaxpr/while/body/eval_jaxpr/ppermute | solution.py:25
  150.2 9.1 %collective-permute-start = (f32[8,1,1024]{2,1,0:T(1,128)}, f32[8,1,1024]{2,1,0:T(1,128)}, u32[]{:S(2)}, u32[]{:S(2)}) collective-permute-start(f32[8,1,1024]{2,1,0:T(1,128)} %get-tuple-element.817), channel_id=1, source_target_pairs={{1,0},{2,1},{3,2},{4,3},{5,4},{6,5},{7,6},{8,7},{9,8},{10,9},{11,1... | collective-permute-start | bytes 98312 | tf_op jit(solution)/shard_map/while/body/eval_jaxpr/while/body/eval_jaxpr/ppermute | solution.py:25
  151.5 7.8 %collective-permute-start.1 = (f32[8,1,1024]{2,1,0:T(1,128)}, f32[8,1,1024]{2,1,0:T(1,128)}, u32[]{:S(2)}, u32[]{:S(2)}) collective-permute-start(f32[8,1,1024]{2,1,0:T(1,128)} %get-tuple-element.818), channel_id=1, source_target_pairs={{0,1},{1,2},{2,3},{3,4},{4,5},{5,6},{6,7},{7,8},{8,9},{9,10},{10,1... | collective-permute-start | bytes 98312 | tf_op jit(solution)/shard_map/while/body/eval_jaxpr/while/body/eval_jaxpr/ppermute | solution.py:22
  162.5 9.6 %collective-permute-start = (f32[8,1,1024]{2,1,0:T(1,128)}, f32[8,1,1024]{2,1,0:T(1,128)}, u32[]{:S(2)}, u32[]{:S(2)}) collective-permute-start(f32[8,1,1024]{2,1,0:T(1,128)} %get-tuple-element.817), channel_id=1, source_target_pairs={{1,0},{2,1},{3,2},{4,3},{5,4},{6,5},{7,6},{8,7},{9,8},{10,9},{11,1... | collective-permute-start | bytes 98312 | tf_op jit(solution)/shard_map/while/body/eval_jaxpr/while/body/eval_jaxpr/ppermute | solution.py:25
  163.8 8.3 %collective-permute-start.1 = (f32[8,1,1024]{2,1,0:T(1,128)}, f32[8,1,1024]{2,1,0:T(1,128)}, u32[]{:S(2)}, u32[]{:S(2)}) collective-permute-start(f32[8,1,1024]{2,1,0:T(1,128)} %get-tuple-element.818), channel_id=1, source_target_pairs={{0,1},{1,2},{2,3},{3,4},{4,5},{5,6},{6,7},{7,8},{8,9},{9,10},{10,1... | collective-permute-start | bytes 98312 | tf_op jit(solution)/shard_map/while/body/eval_jaxpr/while/body/eval_jaxpr/ppermute | solution.py:22
  175.3 9.6 %collective-permute-start = (f32[8,1,1024]{2,1,0:T(1,128)}, f32[8,1,1024]{2,1,0:T(1,128)}, u32[]{:S(2)}, u32[]{:S(2)}) collective-permute-start(f32[8,1,1024]{2,1,0:T(1,128)} %get-tuple-element.817), channel_id=1, source_target_pairs={{1,0},{2,1},{3,2},{4,3},{5,4},{6,5},{7,6},{8,7},{9,8},{10,9},{11,1... | collective-permute-start | bytes 98312 | tf_op jit(solution)/shard_map/while/body/eval_jaxpr/while/body/eval_jaxpr/ppermute | solution.py:25
  176.6 8.3 %collective-permute-start.1 = (f32[8,1,1024]{2,1,0:T(1,128)}, f32[8,1,1024]{2,1,0:T(1,128)}, u32[]{:S(2)}, u32[]{:S(2)}) collective-permute-start(f32[8,1,1024]{2,1,0:T(1,128)} %get-tuple-element.818), channel_id=1, source_target_pairs={{0,1},{1,2},{2,3},{3,4},{4,5},{5,6},{6,7},{7,8},{8,9},{9,10},{10,1... | collective-permute-start | bytes 98312 | tf_op jit(solution)/shard_map/while/body/eval_jaxpr/while/body/eval_jaxpr/ppermute | solution.py:22
  188.1 9.6 %collective-permute-start = (f32[8,1,1024]{2,1,0:T(1,128)}, f32[8,1,1024]{2,1,0:T(1,128)}, u32[]{:S(2)}, u32[]{:S(2)}) collective-permute-start(f32[8,1,1024]{2,1,0:T(1,128)} %get-tuple-element.817), channel_id=1, source_target_pairs={{1,0},{2,1},{3,2},{4,3},{5,4},{6,5},{7,6},{8,7},{9,8},{10,9},{11,1... | collective-permute-start | bytes 98312 | tf_op jit(solution)/shard_map/while/body/eval_jaxpr/while/body/eval_jaxpr/ppermute | solution.py:25
  189.4 8.3 %collective-permute-start.1 = (f32[8,1,1024]{2,1,0:T(1,128)}, f32[8,1,1024]{2,1,0:T(1,128)}, u32[]{:S(2)}, u32[]{:S(2)}) collective-permute-start(f32[8,1,1024]{2,1,0:T(1,128)} %get-tuple-element.818), channel_id=1, source_target_pairs={{0,1},{1,2},{2,3},{3,4},{4,5},{5,6},{6,7},{7,8},{8,9},{9,10},{10,1... | collective-permute-start | bytes 98312 | tf_op jit(solution)/shard_map/while/body/eval_jaxpr/while/body/eval_jaxpr/ppermute | solution.py:22
  200.9 9.6 %collective-permute-start = (f32[8,1,1024]{2,1,0:T(1,128)}, f32[8,1,1024]{2,1,0:T(1,128)}, u32[]{:S(2)}, u32[]{:S(2)}) collective-permute-start(f32[8,1,1024]{2,1,0:T(1,128)} %get-tuple-element.817), channel_id=1, source_target_pairs={{1,0},{2,1},{3,2},{4,3},{5,4},{6,5},{7,6},{8,7},{9,8},{10,9},{11,1... | collective-permute-start | bytes 98312 | tf_op jit(solution)/shard_map/while/body/eval_jaxpr/while/body/eval_jaxpr/ppermute | solution.py:25
  202.2 8.3 %collective-permute-start.1 = (f32[8,1,1024]{2,1,0:T(1,128)}, f32[8,1,1024]{2,1,0:T(1,128)}, u32[]{:S(2)}, u32[]{:S(2)}) collective-permute-start(f32[8,1,1024]{2,1,0:T(1,128)} %get-tuple-element.818), channel_id=1, source_target_pairs={{0,1},{1,2},{2,3},{3,4},{4,5},{5,6},{6,7},{7,8},{8,9},{9,10},{10,1... | collective-permute-start | bytes 98312 | tf_op jit(solution)/shard_map/while/body/eval_jaxpr/while/body/eval_jaxpr/ppermute | solution.py:22
  223.9 9.6 %collective-permute-start = (f32[8,1,1024]{2,1,0:T(1,128)}, f32[8,1,1024]{2,1,0:T(1,128)}, u32[]{:S(2)}, u32[]{:S(2)}) collective-permute-start(f32[8,1,1024]{2,1,0:T(1,128)} %get-tuple-element.817), channel_id=1, source_target_pairs={{1,0},{2,1},{3,2},{4,3},{5,4},{6,5},{7,6},{8,7},{9,8},{10,9},{11,1... | collective-permute-start | bytes 98312 | tf_op jit(solution)/shard_map/while/body/eval_jaxpr/while/body/eval_jaxpr/ppermute | solution.py:25
  225.2 8.3 %collective-permute-start.1 = (f32[8,1,1024]{2,1,0:T(1,128)}, f32[8,1,1024]{2,1,0:T(1,128)}, u32[]{:S(2)}, u32[]{:S(2)}) collective-permute-start(f32[8,1,1024]{2,1,0:T(1,128)} %get-tuple-element.818), channel_id=1, source_target_pairs={{0,1},{1,2},{2,3},{3,4},{4,5},{5,6},{6,7},{7,8},{8,9},{9,10},{10,1... | collective-permute-start | bytes 98312 | tf_op jit(solution)/shard_map/while/body/eval_jaxpr/while/body/eval_jaxpr/ppermute | solution.py:22
  236.7 9.6 %collective-permute-start = (f32[8,1,1024]{2,1,0:T(1,128)}, f32[8,1,1024]{2,1,0:T(1,128)}, u32[]{:S(2)}, u32[]{:S(2)}) collective-permute-start(f32[8,1,1024]{2,1,0:T(1,128)} %get-tuple-element.817), channel_id=1, source_target_pairs={{1,0},{2,1},{3,2},{4,3},{5,4},{6,5},{7,6},{8,7},{9,8},{10,9},{11,1... | collective-permute-start | bytes 98312 | tf_op jit(solution)/shard_map/while/body/eval_jaxpr/while/body/eval_jaxpr/ppermute | solution.py:25
  238.0 8.3 %collective-permute-start.1 = (f32[8,1,1024]{2,1,0:T(1,128)}, f32[8,1,1024]{2,1,0:T(1,128)}, u32[]{:S(2)}, u32[]{:S(2)}) collective-permute-start(f32[8,1,1024]{2,1,0:T(1,128)} %get-tuple-element.818), channel_id=1, source_target_pairs={{0,1},{1,2},{2,3},{3,4},{4,5},{5,6},{6,7},{7,8},{8,9},{9,10},{10,1... | collective-permute-start | bytes 98312 | tf_op jit(solution)/shard_map/while/body/eval_jaxpr/while/body/eval_jaxpr/ppermute | solution.py:22
  249.5 9.6 %collective-permute-start = (f32[8,1,1024]{2,1,0:T(1,128)}, f32[8,1,1024]{2,1,0:T(1,128)}, u32[]{:S(2)}, u32[]{:S(2)}) collective-permute-start(f32[8,1,1024]{2,1,0:T(1,128)} %get-tuple-element.817), channel_id=1, source_target_pairs={{1,0},{2,1},{3,2},{4,3},{5,4},{6,5},{7,6},{8,7},{9,8},{10,9},{11,1... | collective-permute-start | bytes 98312 | tf_op jit(solution)/shard_map/while/body/eval_jaxpr/while/body/eval_jaxpr/ppermute | solution.py:25
  250.8 8.3 %collective-permute-start.1 = (f32[8,1,1024]{2,1,0:T(1,128)}, f32[8,1,1024]{2,1,0:T(1,128)}, u32[]{:S(2)}, u32[]{:S(2)}) collective-permute-start(f32[8,1,1024]{2,1,0:T(1,128)} %get-tuple-element.818), channel_id=1, source_target_pairs={{0,1},{1,2},{2,3},{3,4},{4,5},{5,6},{6,7},{7,8},{8,9},{9,10},{10,1... | collective-permute-start | bytes 98312 | tf_op jit(solution)/shard_map/while/body/eval_jaxpr/while/body/eval_jaxpr/ppermute | solution.py:22
  262.3 9.6 %collective-permute-start = (f32[8,1,1024]{2,1,0:T(1,128)}, f32[8,1,1024]{2,1,0:T(1,128)}, u32[]{:S(2)}, u32[]{:S(2)}) collective-permute-start(f32[8,1,1024]{2,1,0:T(1,128)} %get-tuple-element.817), channel_id=1, source_target_pairs={{1,0},{2,1},{3,2},{4,3},{5,4},{6,5},{7,6},{8,7},{9,8},{10,9},{11,1... | collective-permute-start | bytes 98312 | tf_op jit(solution)/shard_map/while/body/eval_jaxpr/while/body/eval_jaxpr/ppermute | solution.py:25
  263.6 8.3 %collective-permute-start.1 = (f32[8,1,1024]{2,1,0:T(1,128)}, f32[8,1,1024]{2,1,0:T(1,128)}, u32[]{:S(2)}, u32[]{:S(2)}) collective-permute-start(f32[8,1,1024]{2,1,0:T(1,128)} %get-tuple-element.818), channel_id=1, source_target_pairs={{0,1},{1,2},{2,3},{3,4},{4,5},{5,6},{6,7},{7,8},{8,9},{9,10},{10,1... | collective-permute-start | bytes 98312 | tf_op jit(solution)/shard_map/while/body/eval_jaxpr/while/body/eval_jaxpr/ppermute | solution.py:22
  275.1 9.6 %collective-permute-start = (f32[8,1,1024]{2,1,0:T(1,128)}, f32[8,1,1024]{2,1,0:T(1,128)}, u32[]{:S(2)}, u32[]{:S(2)}) collective-permute-start(f32[8,1,1024]{2,1,0:T(1,128)} %get-tuple-element.817), channel_id=1, source_target_pairs={{1,0},{2,1},{3,2},{4,3},{5,4},{6,5},{7,6},{8,7},{9,8},{10,9},{11,1... | collective-permute-start | bytes 98312 | tf_op jit(solution)/shard_map/while/body/eval_jaxpr/while/body/eval_jaxpr/ppermute | solution.py:25
  276.4 8.3 %collective-permute-start.1 = (f32[8,1,1024]{2,1,0:T(1,128)}, f32[8,1,1024]{2,1,0:T(1,128)}, u32[]{:S(2)}, u32[]{:S(2)}) collective-permute-start(f32[8,1,1024]{2,1,0:T(1,128)} %get-tuple-element.818), channel_id=1, source_target_pairs={{0,1},{1,2},{2,3},{3,4},{4,5},{5,6},{6,7},{7,8},{8,9},{9,10},{10,1... | collective-permute-start | bytes 98312 | tf_op jit(solution)/shard_map/while/body/eval_jaxpr/while/body/eval_jaxpr/ppermute | solution.py:22
  287.9 9.6 %collective-permute-start = (f32[8,1,1024]{2,1,0:T(1,128)}, f32[8,1,1024]{2,1,0:T(1,128)}, u32[]{:S(2)}, u32[]{:S(2)}) collective-permute-start(f32[8,1,1024]{2,1,0:T(1,128)} %get-tuple-element.817), channel_id=1, source_target_pairs={{1,0},{2,1},{3,2},{4,3},{5,4},{6,5},{7,6},{8,7},{9,8},{10,9},{11,1... | collective-permute-start | bytes 98312 | tf_op jit(solution)/shard_map/while/body/eval_jaxpr/while/body/eval_jaxpr/ppermute | solution.py:25
  289.2 8.3 %collective-permute-start.1 = (f32[8,1,1024]{2,1,0:T(1,128)}, f32[8,1,1024]{2,1,0:T(1,128)}, u32[]{:S(2)}, u32[]{:S(2)}) collective-permute-start(f32[8,1,1024]{2,1,0:T(1,128)} %get-tuple-element.818), channel_id=1, source_target_pairs={{0,1},{1,2},{2,3},{3,4},{4,5},{5,6},{6,7},{7,8},{8,9},{9,10},{10,1... | collective-permute-start | bytes 98312 | tf_op jit(solution)/shard_map/while/body/eval_jaxpr/while/body/eval_jaxpr/ppermute | solution.py:22
  300.7 9.6 %collective-permute-start = (f32[8,1,1024]{2,1,0:T(1,128)}, f32[8,1,1024]{2,1,0:T(1,128)}, u32[]{:S(2)}, u32[]{:S(2)}) collective-permute-start(f32[8,1,1024]{2,1,0:T(1,128)} %get-tuple-element.817), channel_id=1, source_target_pairs={{1,0},{2,1},{3,2},{4,3},{5,4},{6,5},{7,6},{8,7},{9,8},{10,9},{11,1... | collective-permute-start | bytes 98312 | tf_op jit(solution)/shard_map/while/body/eval_jaxpr/while/body/eval_jaxpr/ppermute | solution.py:25
  302.0 8.3 %collective-permute-start.1 = (f32[8,1,1024]{2,1,0:T(1,128)}, f32[8,1,1024]{2,1,0:T(1,128)}, u32[]{:S(2)}, u32[]{:S(2)}) collective-permute-start(f32[8,1,1024]{2,1,0:T(1,128)} %get-tuple-element.818), channel_id=1, source_target_pairs={{0,1},{1,2},{2,3},{3,4},{4,5},{5,6},{6,7},{7,8},{8,9},{9,10},{10,1... | collective-permute-start | bytes 98312 | tf_op jit(solution)/shard_map/while/body/eval_jaxpr/while/body/eval_jaxpr/ppermute | solution.py:22
  313.5 9.6 %collective-permute-start = (f32[8,1,1024]{2,1,0:T(1,128)}, f32[8,1,1024]{2,1,0:T(1,128)}, u32[]{:S(2)}, u32[]{:S(2)}) collective-permute-start(f32[8,1,1024]{2,1,0:T(1,128)} %get-tuple-element.817), channel_id=1, source_target_pairs={{1,0},{2,1},{3,2},{4,3},{5,4},{6,5},{7,6},{8,7},{9,8},{10,9},{11,1... | collective-permute-start | bytes 98312 | tf_op jit(solution)/shard_map/while/body/eval_jaxpr/while/body/eval_jaxpr/ppermute | solution.py:25
  314.8 8.3 %collective-permute-start.1 = (f32[8,1,1024]{2,1,0:T(1,128)}, f32[8,1,1024]{2,1,0:T(1,128)}, u32[]{:S(2)}, u32[]{:S(2)}) collective-permute-start(f32[8,1,1024]{2,1,0:T(1,128)} %get-tuple-element.818), channel_id=1, source_target_pairs={{0,1},{1,2},{2,3},{3,4},{4,5},{5,6},{6,7},{7,8},{8,9},{9,10},{10,1... | collective-permute-start | bytes 98312 | tf_op jit(solution)/shard_map/while/body/eval_jaxpr/while/body/eval_jaxpr/ppermute | solution.py:22
  336.5 9.6 %collective-permute-start = (f32[8,1,1024]{2,1,0:T(1,128)}, f32[8,1,1024]{2,1,0:T(1,128)}, u32[]{:S(2)}, u32[]{:S(2)}) collective-permute-start(f32[8,1,1024]{2,1,0:T(1,128)} %get-tuple-element.817), channel_id=1, source_target_pairs={{1,0},{2,1},{3,2},{4,3},{5,4},{6,5},{7,6},{8,7},{9,8},{10,9},{11,1... | collective-permute-start | bytes 98312 | tf_op jit(solution)/shard_map/while/body/eval_jaxpr/while/body/eval_jaxpr/ppermute | solution.py:25
  337.8 8.3 %collective-permute-start.1 = (f32[8,1,1024]{2,1,0:T(1,128)}, f32[8,1,1024]{2,1,0:T(1,128)}, u32[]{:S(2)}, u32[]{:S(2)}) collective-permute-start(f32[8,1,1024]{2,1,0:T(1,128)} %get-tuple-element.818), channel_id=1, source_target_pairs={{0,1},{1,2},{2,3},{3,4},{4,5},{5,6},{6,7},{7,8},{8,9},{9,10},{10,1... | collective-permute-start | bytes 98312 | tf_op jit(solution)/shard_map/while/body/eval_jaxpr/while/body/eval_jaxpr/ppermute | solution.py:22
  349.3 9.6 %collective-permute-start = (f32[8,1,1024]{2,1,0:T(1,128)}, f32[8,1,1024]{2,1,0:T(1,128)}, u32[]{:S(2)}, u32[]{:S(2)}) collective-permute-start(f32[8,1,1024]{2,1,0:T(1,128)} %get-tuple-element.817), channel_id=1, source_target_pairs={{1,0},{2,1},{3,2},{4,3},{5,4},{6,5},{7,6},{8,7},{9,8},{10,9},{11,1... | collective-permute-start | bytes 98312 | tf_op jit(solution)/shard_map/while/body/eval_jaxpr/while/body/eval_jaxpr/ppermute | solution.py:25
  350.6 8.3 %collective-permute-start.1 = (f32[8,1,1024]{2,1,0:T(1,128)}, f32[8,1,1024]{2,1,0:T(1,128)}, u32[]{:S(2)}, u32[]{:S(2)}) collective-permute-start(f32[8,1,1024]{2,1,0:T(1,128)} %get-tuple-element.818), channel_id=1, source_target_pairs={{0,1},{1,2},{2,3},{3,4},{4,5},{5,6},{6,7},{7,8},{8,9},{9,10},{10,1... | collective-permute-start | bytes 98312 | tf_op jit(solution)/shard_map/while/body/eval_jaxpr/while/body/eval_jaxpr/ppermute | solution.py:22
  362.1 9.6 %collective-permute-start = (f32[8,1,1024]{2,1,0:T(1,128)}, f32[8,1,1024]{2,1,0:T(1,128)}, u32[]{:S(2)}, u32[]{:S(2)}) collective-permute-start(f32[8,1,1024]{2,1,0:T(1,128)} %get-tuple-element.817), channel_id=1, source_target_pairs={{1,0},{2,1},{3,2},{4,3},{5,4},{6,5},{7,6},{8,7},{9,8},{10,9},{11,1... | collective-permute-start | bytes 98312 | tf_op jit(solution)/shard_map/while/body/eval_jaxpr/while/body/eval_jaxpr/ppermute | solution.py:25
  363.4 8.3 %collective-permute-start.1 = (f32[8,1,1024]{2,1,0:T(1,128)}, f32[8,1,1024]{2,1,0:T(1,128)}, u32[]{:S(2)}, u32[]{:S(2)}) collective-permute-start(f32[8,1,1024]{2,1,0:T(1,128)} %get-tuple-element.818), channel_id=1, source_target_pairs={{0,1},{1,2},{2,3},{3,4},{4,5},{5,6},{6,7},{7,8},{8,9},{9,10},{10,1... | collective-permute-start | bytes 98312 | tf_op jit(solution)/shard_map/while/body/eval_jaxpr/while/body/eval_jaxpr/ppermute | solution.py:22
  374.9 9.6 %collective-permute-start = (f32[8,1,1024]{2,1,0:T(1,128)}, f32[8,1,1024]{2,1,0:T(1,128)}, u32[]{:S(2)}, u32[]{:S(2)}) collective-permute-start(f32[8,1,1024]{2,1,0:T(1,128)} %get-tuple-element.817), channel_id=1, source_target_pairs={{1,0},{2,1},{3,2},{4,3},{5,4},{6,5},{7,6},{8,7},{9,8},{10,9},{11,1... | collective-permute-start | bytes 98312 | tf_op jit(solution)/shard_map/while/body/eval_jaxpr/while/body/eval_jaxpr/ppermute | solution.py:25
  376.2 8.3 %collective-permute-start.1 = (f32[8,1,1024]{2,1,0:T(1,128)}, f32[8,1,1024]{2,1,0:T(1,128)}, u32[]{:S(2)}, u32[]{:S(2)}) collective-permute-start(f32[8,1,1024]{2,1,0:T(1,128)} %get-tuple-element.818), channel_id=1, source_target_pairs={{0,1},{1,2},{2,3},{3,4},{4,5},{5,6},{6,7},{7,8},{8,9},{9,10},{10,1... | collective-permute-start | bytes 98312 | tf_op jit(solution)/shard_map/while/body/eval_jaxpr/while/body/eval_jaxpr/ppermute | solution.py:22
  387.7 9.6 %collective-permute-start = (f32[8,1,1024]{2,1,0:T(1,128)}, f32[8,1,1024]{2,1,0:T(1,128)}, u32[]{:S(2)}, u32[]{:S(2)}) collective-permute-start(f32[8,1,1024]{2,1,0:T(1,128)} %get-tuple-element.817), channel_id=1, source_target_pairs={{1,0},{2,1},{3,2},{4,3},{5,4},{6,5},{7,6},{8,7},{9,8},{10,9},{11,1... | collective-permute-start | bytes 98312 | tf_op jit(solution)/shard_map/while/body/eval_jaxpr/while/body/eval_jaxpr/ppermute | solution.py:25
  389.0 8.3 %collective-permute-start.1 = (f32[8,1,1024]{2,1,0:T(1,128)}, f32[8,1,1024]{2,1,0:T(1,128)}, u32[]{:S(2)}, u32[]{:S(2)}) collective-permute-start(f32[8,1,1024]{2,1,0:T(1,128)} %get-tuple-element.818), channel_id=1, source_target_pairs={{0,1},{1,2},{2,3},{3,4},{4,5},{5,6},{6,7},{7,8},{8,9},{9,10},{10,1... | collective-permute-start | bytes 98312 | tf_op jit(solution)/shard_map/while/body/eval_jaxpr/while/body/eval_jaxpr/ppermute | solution.py:22
  400.5 9.6 %collective-permute-start = (f32[8,1,1024]{2,1,0:T(1,128)}, f32[8,1,1024]{2,1,0:T(1,128)}, u32[]{:S(2)}, u32[]{:S(2)}) collective-permute-start(f32[8,1,1024]{2,1,0:T(1,128)} %get-tuple-element.817), channel_id=1, source_target_pairs={{1,0},{2,1},{3,2},{4,3},{5,4},{6,5},{7,6},{8,7},{9,8},{10,9},{11,1... | collective-permute-start | bytes 98312 | tf_op jit(solution)/shard_map/while/body/eval_jaxpr/while/body/eval_jaxpr/ppermute | solution.py:25
  401.8 8.3 %collective-permute-start.1 = (f32[8,1,1024]{2,1,0:T(1,128)}, f32[8,1,1024]{2,1,0:T(1,128)}, u32[]{:S(2)}, u32[]{:S(2)}) collective-permute-start(f32[8,1,1024]{2,1,0:T(1,128)} %get-tuple-element.818), channel_id=1, source_target_pairs={{0,1},{1,2},{2,3},{3,4},{4,5},{5,6},{6,7},{7,8},{8,9},{9,10},{10,1... | collective-permute-start | bytes 98312 | tf_op jit(solution)/shard_map/while/body/eval_jaxpr/while/body/eval_jaxpr/ppermute | solution.py:22
  413.4 9.6 %collective-permute-start = (f32[8,1,1024]{2,1,0:T(1,128)}, f32[8,1,1024]{2,1,0:T(1,128)}, u32[]{:S(2)}, u32[]{:S(2)}) collective-permute-start(f32[8,1,1024]{2,1,0:T(1,128)} %get-tuple-element.817), channel_id=1, source_target_pairs={{1,0},{2,1},{3,2},{4,3},{5,4},{6,5},{7,6},{8,7},{9,8},{10,9},{11,1... | collective-permute-start | bytes 98312 | tf_op jit(solution)/shard_map/while/body/eval_jaxpr/while/body/eval_jaxpr/ppermute | solution.py:25
  414.6 8.3 %collective-permute-start.1 = (f32[8,1,1024]{2,1,0:T(1,128)}, f32[8,1,1024]{2,1,0:T(1,128)}, u32[]{:S(2)}, u32[]{:S(2)}) collective-permute-start(f32[8,1,1024]{2,1,0:T(1,128)} %get-tuple-element.818), channel_id=1, source_target_pairs={{0,1},{1,2},{2,3},{3,4},{4,5},{5,6},{6,7},{7,8},{8,9},{9,10},{10,1... | collective-permute-start | bytes 98312 | tf_op jit(solution)/shard_map/while/body/eval_jaxpr/while/body/eval_jaxpr/ppermute | solution.py:22
  426.2 9.6 %collective-permute-start = (f32[8,1,1024]{2,1,0:T(1,128)}, f32[8,1,1024]{2,1,0:T(1,128)}, u32[]{:S(2)}, u32[]{:S(2)}) collective-permute-start(f32[8,1,1024]{2,1,0:T(1,128)} %get-tuple-element.817), channel_id=1, source_target_pairs={{1,0},{2,1},{3,2},{4,3},{5,4},{6,5},{7,6},{8,7},{9,8},{10,9},{11,1... | collective-permute-start | bytes 98312 | tf_op jit(solution)/shard_map/while/body/eval_jaxpr/while/body/eval_jaxpr/ppermute | solution.py:25
  427.4 8.3 %collective-permute-start.1 = (f32[8,1,1024]{2,1,0:T(1,128)}, f32[8,1,1024]{2,1,0:T(1,128)}, u32[]{:S(2)}, u32[]{:S(2)}) collective-permute-start(f32[8,1,1024]{2,1,0:T(1,128)} %get-tuple-element.818), channel_id=1, source_target_pairs={{0,1},{1,2},{2,3},{3,4},{4,5},{5,6},{6,7},{7,8},{8,9},{9,10},{10,1... | collective-permute-start | bytes 98312 | tf_op jit(solution)/shard_map/while/body/eval_jaxpr/while/body/eval_jaxpr/ppermute | solution.py:22
  (27 other events, 133.9 us)
Sparse Core Ops, SparseCore 0:
  442.9 53.2 reduce-scatter.1
where the time goes:
time: 507 us; the launch traced here: 503 us
  starting transfers between devices  261 us (51%)
  other arithmetic  106 us (21%)
  waiting for transfers between devices  53.6 us (11%)
  local copies, waits for them, and re-layouts  38.5 us (8%)
  loops' own time  30.6 us (6%)
  between operations  13.4 us (3%)
    ppermute x33, starting transfers between devices, with_halo(): lax.ppermute(lax.slice_in_dim(block, block.shape[dim] - width, None, axis...  218 us
    select_n x32, other arithmetic, chebyshev_step(): jnp.where(active, moved, direction)  67.1 us
    reduce_scatter x1, waiting for transfers between devices, local(): return lax.psum_scatter(summed, 'wave', scatter_dimension=0, tiled=True)  53.4 us
    ppermute x33, starting transfers between devices, with_halo(): lax.ppermute(lax.slice_in_dim(block, 0, width, axis=dim), axis, backward)  42.3 us
    another operation x4, loops' own time, advance(): lax.fori_loop(0, ITERS, sweep, (start, jnp.zeros_like(start), rho_start))[0]  24.6 us
    slice x33, local copies, waits for them, and re-layouts, with_halo(): lax.slice_in_dim(block, block.shape[dim] - width, None, axis=dim)  22.2 us
    select_n x32, other arithmetic, chebyshev_step(): jnp.where(active, field + moved, field)  14.3 us
    dynamic_slice x12, local copies, waits for them, and re-layouts, local(): lax.scan(per_wave, jnp.zeros((source_count, row_count, col_count), jnp.fl...  12.9 us
  transfers between devices with their start and end apart: 67, of which 1 were waited for; matrix products, arithmetic and copies ran while one was open for 1% of the time, Pallas kernels for 0%

commit v1 on v0

v1 whole, which is shorter than its diff:
```python
import functools

import jax
import jax.numpy as jnp
from jax import lax
from jax.experimental import pallas as pl
from jax.experimental.pallas import tpu as pltpu
from jax.sharding import PartitionSpec as P

ITERS = 8
LOWER = 0.1
UPPER = 2.0
THETA = (UPPER + LOWER) / 2.0
DELTA = (UPPER - LOWER) / 2.0
SIGMA_ONE = THETA / DELTA
CURRENT = 2.0

TAU = [1.0, SIGMA_ONE]
for _ in range(ITERS):
    TAU.append(2.0 * SIGMA_ONE * TAU[-1] - TAU[-2])
OMEGA = 2.0 * (THETA - 1.0) / DELTA

LANES = 128
ROWS = 32
PAD = 16
SPAN = ROWS + 2 * PAD
SWEEP_ROWS = ((8, 6), (8, 6), (8, 6), (12, 5), (12, 5), (12, 5), (12, 5), (16, 4))
MESH = pl.DeviceIdType.MESH


def chosen(index, table):
    value = jnp.float32(0.0)
    for position, entry in enumerate(table):
        value = jnp.where(index == position, jnp.float32(entry), value)
    return value


def slot_column(pair, half, wave_pos):
    middle = jnp.logical_or(pair == 1, pair == 2)
    ahead = jnp.where(pair == 0, 2, jnp.where(middle, 1 + 2 * half, 0))
    offset = jnp.where(middle, pair - 1, half)
    return 2 * lax.rem(wave_pos + ahead, 4) + offset


def kernel(
    fields, sigma, wavenumbers, weights, counts, electrodes, pairs, out,
    halo_n, halo_s, sig_n, sig_s, sig, w, coef, gain, src, acc, from_low, from_high,
    omegas, charges, finals, h_send, h_recv, s_send, s_recv, r_send, r_recv,
):
    per_group = fields.shape[0]
    tiles = fields.shape[3] // LANES
    tile_count = lax.axis_size("tile")
    wave_count = lax.axis_size("wave")
    tile_pos = lax.axis_index("tile")
    wave_pos = lax.axis_index("wave")
    south = {"tile": lax.rem(tile_pos + 1, tile_count)}
    north = {"tile": lax.rem(tile_pos + tile_count - 1, tile_count)}
    above = {"wave": lax.rem(wave_pos + 1, wave_count)}
    below = {"wave": lax.rem(wave_pos + wave_count - 1, wave_count)}

    barrier = pltpu.get_barrier_semaphore()
    for other in (south, north, above, below):
        pl.semaphore_signal(barrier, inc=1, device_id=other, device_id_type=MESH)
    pl.semaphore_wait(barrier, 4)

    def remote(source, target, send, recv, device):
        return pltpu.make_async_remote_copy(
            src_ref=source, dst_ref=target, send_sem=send, recv_sem=recv,
            device_id=device, device_id_type=MESH,
        )

    sig_south = remote(sigma.at[pl.ds(ROWS - 8, 8)], sig_n, s_send.at[0], s_recv.at[0], south)
    sig_north = remote(sigma.at[pl.ds(0, 8)], sig_s, s_send.at[1], s_recv.at[1], north)
    sig_south.start()
    sig_north.start()

    def halo_copies(slot, k):
        column = slot_column(slot // 2, lax.rem(slot, 2), wave_pos)
        return (
            remote(fields.at[k, column, pl.ds(ROWS - 16, 16)], halo_n.at[slot, k],
                   h_send.at[0, slot, k], h_recv.at[0, slot, k], south),
            remote(fields.at[k, column, pl.ds(0, 16)], halo_s.at[slot, k],
                   h_send.at[1, slot, k], h_recv.at[1, slot, k], north),
        )

    @pl.loop(0, 4)
    def _(pair):
        @pl.loop(0, per_group)
        def _(k):
            for half in range(2):
                for copy in halo_copies(2 * pair + half, k):
                    copy.start()

    for k in range(per_group):
        count = counts[wave_pos * per_group + k]
        for step in range(ITERS):
            live = step - (ITERS - count)
            omegas[k * ITERS + step] = jnp.where(
                live < 0, jnp.float32(2.0),
                jnp.where(live == 0, jnp.float32(1.0 + 0.5 * OMEGA), jnp.float32(OMEGA)))
            charges[k * ITERS + step] = chosen(live, [0.5] + TAU[1:ITERS])
        finals[k] = weights[wave_pos * per_group + k] * chosen(
            count, [1.0 / tau for tau in TAU[: ITERS + 1]])

    lane = lax.broadcasted_iota(jnp.int32, (8, LANES), 1)
    sub = lax.broadcasted_iota(jnp.int32, (8, LANES), 0)
    first_lane = lane == 0
    last_lane = lane == LANES - 1
    zero = jnp.zeros((8, LANES), jnp.float32)

    for tile in range(tiles):
        for edge in (0, SPAN - 8):
            sig[tile, pl.ds(edge, 8), :] = zero + 1.0
            for half in range(2):
                for buf in range(2):
                    w[buf, half, tile, pl.ds(edge, 8), :] = zero
        for row in range(8, SPAN - 8, 8):
            for face in range(4):
                coef[0, face, tile, pl.ds(row, 8), :] = zero
        for row in range(0, ROWS, 8):
            sig[tile, pl.ds(PAD + row, 8), :] = sigma[pl.ds(row, 8), pl.ds(tile * LANES, LANES)]
            for slot in range(8):
                acc[slot, tile, pl.ds(row, 8), :] = zero
    sig_south.wait_recv()
    sig_north.wait_recv()
    for tile in range(tiles):
        sig[tile, pl.ds(8, 8), :] = sig_n[:, pl.ds(tile * LANES, LANES)]
        sig[tile, pl.ds(PAD + ROWS, 8), :] = sig_s[:, pl.ds(tile * LANES, LANES)]

    def beside(values, tile):
        left = pltpu.roll(values[tile], 1, 1)
        right = pltpu.roll(values[tile], LANES - 1, 1)
        if tile > 0:
            left = jnp.where(first_lane, pltpu.roll(values[tile - 1], 1, 1), left)
        if tile < tiles - 1:
            right = jnp.where(last_lane, pltpu.roll(values[tile + 1], LANES - 1, 1), right)
        return left, right

    @pl.loop(1, SPAN // 8 - 1)
    def _(row_tile):
        row = pl.multiple_of(row_tile * 8, 8)
        place = tile_pos * ROWS + row - PAD + sub
        top = place == 0
        bottom = place == tile_count * ROWS - 1
        centre = [sig[tile, pl.ds(row, 8), :] for tile in range(tiles)]
        for tile in range(tiles):
            mid = centre[tile]
            left, right = beside(centre, tile)
            up = jnp.where(top, 0.0, sig[tile, pl.ds(row - 1, 8), :])
            down = jnp.where(bottom, 0.0, sig[tile, pl.ds(row + 1, 8), :])
            if tile == 0:
                left = jnp.where(first_lane, 0.0, left)
            if tile == tiles - 1:
                right = jnp.where(last_lane, 0.0, right)
            faces = [0.5 * (mid + near) for near in (up, down, left, right)]
            diagonal = (faces[0] + faces[1]) + (faces[2] + faces[3])
            faces[0] = jnp.where(top, 0.0, faces[0])
            faces[1] = jnp.where(bottom, 0.0, faces[1])
            if tile == 0:
                faces[2] = jnp.where(first_lane, 0.0, faces[2])
            if tile == tiles - 1:
                faces[3] = jnp.where(last_lane, 0.0, faces[3])
            for k in range(per_group):
                number = wavenumbers[wave_pos * per_group + k]
                scale = (2.0 / DELTA) / (diagonal + (number * number) * mid)
                if tile == 0:
                    gain[k, pl.ds(row, 8), :] = scale
                for face in range(4):
                    value = faces[face] * scale
                    coef[2 + 2 * k, face, tile, pl.ds(row, 8), :] = value
                    coef[1 + 2 * k, face, tile, pl.ds(row, 8), :] = 0.5 * value

    def sweep(step, k, pair):
        start, count = SWEEP_ROWS[step]
        now, later = step % 2, (step + 1) % 2
        live = step - (ITERS - counts[wave_pos * per_group + k])
        table = jnp.where(live < 0, 0, jnp.where(live == 0, 1 + 2 * k, 2 + 2 * k))
        omega = omegas[k * ITERS + step]
        charge = charges[k * ITERS + step]
        final = finals[k]

        for row_tile in range(count):
            row = start + 8 * row_tile
            centre = [[w[now, half, tile, pl.ds(row, 8), :] for tile in range(tiles)] for half in range(2)]
            for tile in range(tiles):
                c_n, c_s, c_w, c_e = [coef[table, face, tile, pl.ds(row, 8), :] for face in range(4)]
                for half in range(2):
                    mid = centre[half][tile]
                    left, right = beside(centre[half], tile)
                    before = mid if step == 0 else w[later, half, tile, pl.ds(row, 8), :]
                    up = w[now, half, tile, pl.ds(row - 1, 8), :]
                    down = w[now, half, tile, pl.ds(row + 1, 8), :]
                    value = ((omega * mid - before) + (c_n * up + c_s * down)) + (c_w * left + c_e * right)
                    if tile == 0:
                        value = value + charge * src[half, pl.ds(row, 8), :]
                    if step == ITERS - 1:
                        acc[2 * pair + half, tile, pl.ds(row - PAD, 8), :] += final * value
                    else:
                        w[later, half, tile, pl.ds(row, 8), :] = value

    def rs_copies(pair):
        slot = 2 * pair
        return (
            remote(acc.at[slot], from_low.at[pair], r_send.at[0, pair], r_recv.at[0, pair], above),
            remote(acc.at[slot + 1], from_high.at[pair], r_send.at[1, pair], r_recv.at[1, pair], below),
        )

    @pl.loop(0, 4)
    def _(pair):
        columns = [slot_column(pair, half, wave_pos) for half in range(2)]

        @pl.loop(0, per_group)
        def _(k):
            for half in range(2):
                for copy in halo_copies(2 * pair + half, k):
                    copy.wait_recv()
            for half in range(2):
                slot = 2 * pair + half
                low = electrodes[pairs[columns[half], 0]] - tile_pos * ROWS + PAD
                high = electrodes[pairs[columns[half], 1]] - tile_pos * ROWS + PAD
                for row in range(8, SPAN - 8, 8):
                    spot = jnp.where(row + sub == low, CURRENT, 0.0) - jnp.where(row + sub == high, CURRENT, 0.0)
                    src[half, pl.ds(row, 8), :] = jnp.where(first_lane, spot * gain[k, pl.ds(row, 8), :], 0.0)
                for tile in range(tiles):
                    cut = pl.ds(tile * LANES, LANES)
                    w[0, half, tile, pl.ds(8, 8), :] = halo_n[slot, k, :, cut].astype(jnp.float32)[8:]
                    for row in range(0, ROWS, 16):
                        w[0, half, tile, pl.ds(PAD + row, 16), :] = fields[
                            k, columns[half], pl.ds(row, 16), cut].astype(jnp.float32)
                    w[0, half, tile, pl.ds(PAD + ROWS, 8), :] = halo_s[slot, k, :, cut].astype(jnp.float32)[:8]
            for step in range(ITERS):
                sweep(step, k, pair)

        @pl.when(pair == 1)
        def _():
            rs_copies(0)[0].wait_recv()
            acc[2] += from_low[0]

        @pl.when(pair == 2)
        def _():
            rs_copies(0)[1].wait_recv()
            acc[5] += from_high[0]

        @pl.when(pair < 3)
        def _():
            for copy in rs_copies(pair):
                copy.start()

    for pair in (1, 2):
        for copy in rs_copies(pair):
            copy.wait_recv()
    for half in range(2):
        for tile in range(tiles):
            for row in range(0, ROWS, 8):
                cut = pl.ds(row, 8)
                out[half, cut, pl.ds(tile * LANES, LANES)] = (
                    acc[6 + half, tile, cut, :] + (from_low[1 + half, tile, cut, :] + from_high[1 + half, tile, cut, :]))

    for pair in range(3):
        for copy in rs_copies(pair):
            copy.wait_send()
    sig_south.wait_send()
    sig_north.wait_send()

    @pl.loop(0, 8)
    def _(slot):
        @pl.loop(0, per_group)
        def _(k):
            for copy in halo_copies(slot, k):
                copy.wait_send()


def local(fields, sigma, wavenumbers, weights, counts, electrodes, pairs):
    per_group, sources, rows, depth = fields.shape
    tiles = depth // LANES
    vmem = pl.BlockSpec(memory_space=pltpu.VMEM)
    smem = pl.BlockSpec(memory_space=pltpu.SMEM)
    f32 = jnp.float32
    return pl.pallas_call(
        kernel,
        out_shape=jax.ShapeDtypeStruct((sources // 4, rows, depth), f32),
        in_specs=[vmem, vmem, smem, smem, smem, smem, smem],
        out_specs=vmem,
        scratch_shapes=[
            pltpu.VMEM((sources, per_group, 16, depth), jnp.bfloat16),
            pltpu.VMEM((sources, per_group, 16, depth), jnp.bfloat16),
            pltpu.VMEM((8, depth), f32),
            pltpu.VMEM((8, depth), f32),
            pltpu.VMEM((tiles, SPAN, LANES), f32),
            pltpu.VMEM((2, 2, tiles, SPAN, LANES), f32),
            pltpu.VMEM((1 + 2 * per_group, 4, tiles, SPAN, LANES), f32),
            pltpu.VMEM((per_group, SPAN, LANES), f32),
            pltpu.VMEM((2, SPAN, LANES), f32),
            pltpu.VMEM((sources, tiles, rows, LANES), f32),
            pltpu.VMEM((3, tiles, rows, LANES), f32),
            pltpu.VMEM((3, tiles, rows, LANES), f32),
            pltpu.SMEM((per_group * ITERS,), f32),
            pltpu.SMEM((per_group * ITERS,), f32),
            pltpu.SMEM((per_group,), f32),
            pltpu.SemaphoreType.DMA((2, sources, per_group)),
            pltpu.SemaphoreType.DMA((2, sources, per_group)),
            pltpu.SemaphoreType.DMA((2,)),
            pltpu.SemaphoreType.DMA((2,)),
            pltpu.SemaphoreType.DMA((2, 3)),
            pltpu.SemaphoreType.DMA((2, 3)),
        ],
        compiler_params=pltpu.CompilerParams(
            collective_id=0, has_side_effects=True, vmem_limit_bytes=40 * 1024 * 1024),
    )(fields, sigma, wavenumbers, weights, counts, electrodes, pairs)


def solution(mesh):
    placed = (P("wave", None, "tile", None), P("tile", None), P(), P(), P(), P(), P())
    return jax.shard_map(
        local, mesh=mesh, in_specs=placed, out_specs=P("wave", "tile", None), check_vma=False
    )
```

time: 507 us -> 53.4 us (0.11)
  starting transfers between devices: 261 us -> 0 us
  other arithmetic: 106 us -> 0 us
  waiting for transfers between devices: 53.6 us -> 0 us
  Pallas kernels: 0 us -> 46.7 us
  local copies, waits for them, and re-layouts: 38.5 us -> 6.57 us
  loops' own time: 30.6 us -> 0 us
  between operations: 13.4 us -> 0.02 us
    ppermute x66 -> x0, starting transfers between devices: 261 us -> none  [the longest x33 218 us: with_halo(): lax.ppermute(lax.slice_in_dim(block, block.shape[dim] - width, None, axis...]
    select_n x96 -> x0, other arithmetic: 81.7 us -> none  [the longest x32 67.1 us: chebyshev_step(): jnp.where(active, moved, direction)]
    reduce_scatter x1 -> x0, waiting for transfers between devices: 53.4 us -> none  [local(): return lax.psum_scatter(summed, 'wave', scatter_dimension=0, tiled=True)]
    pallas_call x0 -> x1, Pallas kernels: none -> 46.7 us  [local(): pl.pallas_call(kernel, out_shape=jax.ShapeDtypeStruct((sources // 4, rows...]
    another operation x5 -> x0, loops' own time: 30.6 us -> none  [the longest x4 24.6 us: advance(): lax.fori_loop(0, ITERS, sweep, (start, jnp.zeros_like(start), rho_start))[0]]
    slice x34 -> x0, local copies, waits for them, and re-layouts: 22.2 us -> none  [the longest x33 22.2 us: with_halo(): lax.slice_in_dim(block, block.shape[dim] - width, None, axis=dim)]
    add x10 -> x0, other arithmetic: 17.1 us -> none  [the longest x4 11.3 us: per_wave(): return (total + weight * solved, None)]
    dynamic_slice x15 -> x0, local copies, waits for them, and re-layouts: 16.1 us -> none  [the longest x12 12.9 us: local(): lax.scan(per_wave, jnp.zeros((source_count, row_count, col_count), jnp.fl...]
  transfers between devices with their start and end apart: 67 -> 0, of which waited for: 1 -> 0; matrix products, arithmetic and copies ran while one was open for 1% -> 0% of each run, Pallas kernels for 0% -> 0%
where the time goes in v1:
time: 53.4 us; the launch traced here: 53.2 us
  Pallas kernels  46.7 us (87%)
  local copies, waits for them, and re-layouts  6.57 us (12%)
    pallas_call x1, Pallas kernels, local(): pl.pallas_call(kernel, out_shape=jax.ShapeDtypeStruct((sources // 4, rows...  46.7 us
    unnamed x14, local copies, waits for them, and re-layouts  6.57 us

profile of v1, /device:TPU:0, one launch (start us, length us, event | category | flops | bytes accessed | tf_op | source)
XLA Modules:
  0.0 53.2 jit_solution(6844327576465561935)
XLA Ops:
  0.0 0.8 %copy.8.pairs = s32[8,2]{1,0:T(8,128)S(1)} copy(s32[8,2]{0,1:T(2,128)} %param.13) | data formatting | bytes 128 | tf_op args[6]
  0.8 0.0 copy-start
  0.8 1.6 %copy-done = bf16[4,8,32,1024]{3,2,1,0:T(8,128)(2,1)S(1)} copy-done((bf16[4,8,32,1024]{3,2,1,0:T(8,128)(2,1)S(1)}, bf16[4,8,32,1024]{3,2,1,0:T(8,128)(2,1)}, u32[]{:S(2)}) %copy-start) | copy-done | bytes 2097176
  2.3 0.0 copy-start.1
  2.3 0.9 %copy-done.1 = f32[32,1024]{1,0:T(8,128)S(1)} copy-done((f32[32,1024]{1,0:T(8,128)S(1)}, f32[32,1024]{1,0:T(8,128)}, u32[]{:S(2)}) %copy-start.1) | copy-done | bytes 131096
  3.2 0.0 copy-start.2
  3.3 0.7 %copy-done.2 = f32[16]{0:T(128)S(1)} copy-done((f32[16]{0:T(128)S(1)}, f32[16]{0:T(128)}, u32[]{:S(2)}) %copy-start.2) | copy-done | bytes 88
  3.9 0.0 copy-start.3
  3.9 0.7 %copy-done.3 = f32[16]{0:T(128)S(1)} copy-done((f32[16]{0:T(128)S(1)}, f32[16]{0:T(128)}, u32[]{:S(2)}) %copy-start.3) | copy-done | bytes 88
  4.6 0.0 copy-start.4
  4.6 0.7 %copy-done.4 = s32[16]{0:T(128)S(1)} copy-done((s32[16]{0:T(128)S(1)}, s32[16]{0:T(128)}, u32[]{:S(2)}) %copy-start.4) | copy-done | bytes 88
  5.2 0.0 copy-start.5
  5.2 0.7 %copy-done.5 = s32[64]{0:T(128)S(1)} copy-done((s32[64]{0:T(128)S(1)}, s32[64]{0:T(128)}, u32[]{:S(2)}) %copy-start.5) | copy-done | bytes 280
  5.9 46.7 %shard_map.73 = f32[2,32,1024]{2,1,0:T(8,128)S(1)} custom-call(bf16[4,8,32,1024]{3,2,1,0:T(8,128)(2,1)S(1)} %copy-done, f32[32,1024]{1,0:T(8,128)S(1)} %copy-done.1, f32[16]{0:T(128)S(1)} %copy-done.2, f32[16]{0:T(128)S(1)} %copy-done.3, s32[16]{0:T(128)S(1)} %copy-done.4, s32[64]{0:T(128)S(1)} %copy-done.5, s32[8,2]{1,0:T(8,128)S(1)} %copy.8.pairs), custom_call_target="tpu_custom_call" | custom-call | tf_op jit(solution)/shard_map/pallas_call | solution.py:279
  52.5 0.7 %copy.10 = f32[2,32,1024]{2,1,0:T(8,128)} copy(f32[2,32,1024]{2,1,0:T(8,128)S(1)} %shard_map.73) | data formatting | bytes 524288
Async XLA Ops:
  0.8 1.6 %copy-start = (bf16[4,8,32,1024]{3,2,1,0:T(8,128)(2,1)S(1)}, bf16[4,8,32,1024]{3,2,1,0:T(8,128)(2,1)}, u32[]{:S(2)}) copy-start(bf16[4,8,32,1024]{3,2,1,0:T(8,128)(2,1)} %fields.1) | copy-start | bytes 6291460
  2.3 0.9 %copy-start.1 = (f32[32,1024]{1,0:T(8,128)S(1)}, f32[32,1024]{1,0:T(8,128)}, u32[]{:S(2)}) copy-start(f32[32,1024]{1,0:T(8,128)} %sigma.1) | copy-start | bytes 393220
  3.2 0.7 %copy-start.2 = (f32[16]{0:T(128)S(1)}, f32[16]{0:T(128)}, u32[]{:S(2)}) copy-start(f32[16]{0:T(128)} %wavenumbers.1) | copy-start | bytes 196
  3.9 0.7 %copy-start.3 = (f32[16]{0:T(128)S(1)}, f32[16]{0:T(128)}, u32[]{:S(2)}) copy-start(f32[16]{0:T(128)} %weights.1) | copy-start | bytes 196
  4.6 0.7 %copy-start.4 = (s32[16]{0:T(128)S(1)}, s32[16]{0:T(128)}, u32[]{:S(2)}) copy-start(s32[16]{0:T(128)} %counts.1) | copy-start | bytes 196
  5.2 0.7 %copy-start.5 = (s32[64]{0:T(128)S(1)}, s32[64]{0:T(128)}, u32[]{:S(2)}) copy-start(s32[64]{0:T(128)} %electrodes.1) | copy-start | bytes 772

commit v2 on v0

v2 whole, which is shorter than its diff:
```python
import jax
import jax.numpy as jnp
from jax import lax
from jax.experimental import pallas as pl
from jax.experimental.pallas import tpu as pltpu
from jax.sharding import PartitionSpec as P

ITERS = 8
LOWER = 0.1
UPPER = 2.0
THETA = (UPPER + LOWER) / 2.0
DELTA = (UPPER - LOWER) / 2.0
SIGMA_ONE = THETA / DELTA
CURRENT = 2.0

TAU = [1.0, SIGMA_ONE]
for _ in range(ITERS):
    TAU.append(2.0 * SIGMA_ONE * TAU[-1] - TAU[-2])
OMEGA = 2.0 * (THETA - 1.0) / DELTA

LANES = 128
SUBS = 8
PARTS = 8
ROWS = 32
HALO = 8
HELD = ROWS + 2 * HALO
SPAN = 64
FIRST = 8
CORE = FIRST + HALO
LAST = FIRST + HELD
UNROLL = 4
MESH = pl.DeviceIdType.MESH
F32 = jnp.float32
BF16 = jnp.bfloat16


def chosen(index, table):
    value = jnp.float32(0.0)
    for position, entry in enumerate(table):
        value = jnp.where(index == position, jnp.float32(entry), value)
    return value


def slot_column(pair, half, wave_pos):
    middle = jnp.logical_or(pair == 1, pair == 2)
    ahead = jnp.where(pair == 0, 2, jnp.where(middle, 1 + 2 * half, 0))
    offset = jnp.where(middle, pair - 1, half)
    return 2 * lax.rem(wave_pos + ahead, 4) + offset


def thirds(values):
    high = values.astype(BF16)
    rest = values - high.astype(F32)
    middle = rest.astype(BF16)
    low = (rest - middle.astype(F32)).astype(BF16)
    return high, middle, low


def kernel(
    fields_in, sigma_in, wavenumbers_in, weights_in, counts_in, electrodes_in, pairs_in, out,
    fields, sigma, wavenumbers, weights, counts, electrodes, pairs,
    into, back, stage, sig_n, sig_s, sig, diag, face_n, face_w,
    an, aw, root, inverse, vectors, src, w, zbuf, acc, from_low, from_high,
    in_sem, h_send, h_recv, s_send, s_recv, r_send, r_recv,
):
    per_group = fields.shape[0]
    tile_count = lax.axis_size("tile")
    wave_count = lax.axis_size("wave")
    tile_pos = lax.axis_index("tile")
    wave_pos = lax.axis_index("wave")
    south = {"tile": lax.rem(tile_pos + 1, tile_count)}
    north = {"tile": lax.rem(tile_pos + tile_count - 1, tile_count)}
    above = {"wave": lax.rem(wave_pos + 1, wave_count)}
    below = {"wave": lax.rem(wave_pos + wave_count - 1, wave_count)}

    barrier = pltpu.get_barrier_semaphore()
    for other in (south, north, above, below):
        pl.semaphore_signal(barrier, inc=1, device_id=other, device_id_type=MESH)

    loads = [
        pltpu.make_async_copy(source, target, in_sem.at[place])
        for place, (source, target) in enumerate((
            (fields_in, fields), (sigma_in, sigma), (wavenumbers_in, wavenumbers), (weights_in, weights),
            (counts_in, counts), (electrodes_in, electrodes), (pairs_in, pairs)))
    ]
    for load in loads:
        load.start()

    lane = lax.broadcasted_iota(jnp.int32, (SUBS, LANES), 1)
    sub = lax.broadcasted_iota(jnp.int32, (SUBS, LANES), 0)
    first_lane = lane == 0
    last_lane = lane == LANES - 1
    zero = jnp.zeros((SUBS, LANES), F32)

    @pl.loop(0, PARTS)
    def _(block):
        wide = PARTS * LANES
        base = pl.multiple_of(block * LANES, LANES)
        row = lax.broadcasted_iota(jnp.int32, (LANES, wide), 0) + base
        column = lax.broadcasted_iota(jnp.int32, (LANES, wide), 1)
        into[pl.ds(base, LANES), :] = jnp.where(
            row == lax.rem(column, LANES) * PARTS + lax.div(column, LANES), 1.0, 0.0).astype(BF16)
        back[pl.ds(base, LANES), :] = jnp.where(
            column == lax.rem(row, LANES) * PARTS + lax.div(row, LANES), 1.0, 0.0).astype(BF16)

    for part in range(PARTS):
        rows8 = pl.ds(part * SUBS, SUBS)
        for row in range(LAST, SPAN):
            an[row, rows8, :] = zero
            aw[row, rows8, :] = zero
            src[row] = zero
            for buf in range(2):
                w[buf, row, rows8, :] = zero
        for edge in (0, LAST):
            sig[part, pl.ds(edge, FIRST), :] = zero + 1.0

    for load in loads:
        load.wait()
    pl.semaphore_wait(barrier, 4)

    def remote(source, target, send, recv, device):
        return pltpu.make_async_remote_copy(
            src_ref=source, dst_ref=target, send_sem=send, recv_sem=recv,
            device_id=device, device_id_type=MESH,
        )

    sig_south = remote(sigma.at[pl.ds(ROWS - HALO, HALO)], sig_n, s_send.at[0], s_recv.at[0], south)
    sig_north = remote(sigma.at[pl.ds(0, HALO)], sig_s, s_send.at[1], s_recv.at[1], north)
    sig_south.start()
    sig_north.start()

    def halo_copies(pair):
        return (
            remote(stage.at[pair, :, :, pl.ds(ROWS, HALO)], stage.at[pair, :, :, pl.ds(0, HALO)],
                   h_send.at[0, pair], h_recv.at[0, pair], south),
            remote(stage.at[pair, :, :, pl.ds(HALO, HALO)], stage.at[pair, :, :, pl.ds(HALO + ROWS, HALO)],
                   h_send.at[1, pair], h_recv.at[1, pair], north),
        )

    @pl.loop(0, 4)
    def _(pair):
        columns = [slot_column(pair, half, wave_pos) for half in range(2)]
        block = jnp.concatenate(
            [fields[k, columns[half]] for half in range(2) for k in range(per_group)], axis=0)
        moved = jnp.dot(block, into[...], preferred_element_type=F32)
        for part in range(PARTS):
            for place in range(SUBS):
                stage[pair, part, place, pl.ds(HALO, ROWS), :] = moved[
                    place * ROWS:(place + 1) * ROWS, part * LANES:(part + 1) * LANES]
        for copy in halo_copies(pair):
            copy.start()

    def by_wavenumber(scalars):
        value = zero
        for k, scalar in enumerate(scalars):
            value = jnp.where(lax.rem(sub, per_group) == k, scalar, value)
        return value

    group = [wave_pos * per_group + k for k in range(per_group)]
    square = by_wavenumber([wavenumbers[g] * wavenumbers[g] for g in group])
    final = by_wavenumber([
        weights[g] * chosen(counts[g], [1.0 / tau for tau in TAU[: ITERS + 1]]) for g in group])
    for step in range(ITERS):
        live = [step - (ITERS - counts[g]) for g in group]
        vectors[3 * step] = by_wavenumber([
            jnp.where(at < 0, F32(2.0), jnp.where(at == 0, F32(1.0 + 0.5 * OMEGA), F32(OMEGA))) for at in live])
        vectors[3 * step + 1] = by_wavenumber([
            jnp.where(at < 0, F32(0.0), jnp.where(at == 0, F32(0.5), F32(1.0))) for at in live])
        vectors[3 * step + 2] = by_wavenumber([chosen(at, [0.5] + TAU[1:ITERS]) for at in live])

    sig_south.wait_recv()
    sig_north.wait_recv()
    whole = jnp.concatenate([sig_n[...], sigma[...], sig_s[...]], axis=0)
    moved = jnp.dot(jnp.concatenate(thirds(whole), axis=0), into[...], preferred_element_type=F32)
    moved = (moved[:HELD] + moved[HELD:2 * HELD]) + moved[2 * HELD:]
    for part in range(PARTS):
        sig[part, pl.ds(FIRST, HELD), :] = moved[:, part * LANES:(part + 1) * LANES]

    @pl.loop(1, LAST // SUBS)
    def _(row_tile):
        row = pl.multiple_of(row_tile * SUBS, SUBS)
        place = tile_pos * ROWS + row - CORE + sub
        last_row = tile_count * ROWS
        centre = [sig[part, pl.ds(row, SUBS), :] for part in range(PARTS)]
        for part in range(PARTS):
            mid = centre[part]
            up = jnp.where(place == 0, 0.0, sig[part, pl.ds(row - 1, SUBS), :])
            down = jnp.where(place == last_row - 1, 0.0, sig[part, pl.ds(row + 1, SUBS), :])
            if part == 0:
                left = jnp.where(first_lane, 0.0, pltpu.roll(centre[-1], 1, 1))
            else:
                left = centre[part - 1]
            if part == PARTS - 1:
                right = jnp.where(last_lane, 0.0, pltpu.roll(centre[0], LANES - 1, 1))
            else:
                right = centre[part + 1]
            faces = [0.5 * (mid + near) for near in (up, down, left, right)]
            diag[part, pl.ds(row, SUBS), :] = (faces[0] + faces[1]) + (faces[2] + faces[3])
            outside = jnp.logical_or(place == 0, place == last_row)
            face_n[part, pl.ds(row, SUBS), :] = jnp.where(outside, 0.0, (2.0 / DELTA) * faces[0])
            west = (2.0 / DELTA) * faces[2]
            if part == 0:
                west = jnp.where(first_lane, 0.0, west)
            face_w[part, pl.ds(row, SUBS), :] = west

    def couplings(row, above_row):
        def spread(ref, part):
            return jnp.broadcast_to(ref[part, pl.ds(row, 1), :], (SUBS, LANES))

        here = []
        for part in range(PARTS):
            rows8 = pl.ds(part * SUBS, SUBS)
            value = spread(diag, part) + square * spread(sig, part)
            guess = lax.rsqrt(value)
            guess = guess * (1.5 - (0.5 * value) * (guess * guess))
            root[row, rows8, :] = value * guess
            inverse[row, rows8, :] = guess
            an[row, rows8, :] = spread(face_n, part) * (guess * above_row[part])
            here.append(guess)
        for part in range(PARTS):
            beside = here[part - 1] if part else pltpu.roll(here[-1], 1, 1)
            aw[row, pl.ds(part * SUBS, SUBS), :] = spread(face_w, part) * (here[part] * beside)
        return tuple(here)

    lax.fori_loop(FIRST, LAST, couplings, (zero,) * PARTS)

    def sweep(step):
        now, later = step % 2, (step + 1) % 2
        before = now if step == 0 else later
        centre_gain = vectors[3 * step]
        side_gain = vectors[3 * step + 1]
        charge = vectors[3 * step + 2]
        start = FIRST + step + 1
        blocks = -(-(HELD - 1 - 2 * step) // UNROLL)
        parts = [pl.ds(part * SUBS, SUBS) for part in range(PARTS)]

        def one(row, carry):
            old, sums = carry
            u = [w[now, row, at, :] for at in parts]
            north_c = [an[row, at, :] for at in parts]
            west_c = [aw[row, at, :] for at in parts]
            for part, at in enumerate(parts):
                value = side_gain * (sums[part] + north_c[part] * u[part]) + (
                    centre_gain * old[part] - w[before, row - 1, at, :])
                if part == 0:
                    value = value + charge * src[row - 1]
                w[later, row - 1, at, :] = value
            flows = [west_c[part] * u[part] for part in range(PARTS)]
            left = [pltpu.roll(u[-1], 1, 1)] + u[:-1]
            right = flows[1:] + [pltpu.roll(flows[0], LANES - 1, 1)]
            sums = [north_c[part] * old[part] + (west_c[part] * left[part] + right[part]) for part in range(PARTS)]
            return tuple(u), tuple(sums)

        def body(block, carry):
            for place in range(UNROLL):
                carry = one(start + UNROLL * block + place, carry)
            return carry

        opening = tuple(w[now, start - 1, at, :] for at in parts)
        lax.fori_loop(0, blocks, body, (opening, (zero,) * PARTS))

    def rs_copies(pair):
        slot = 2 * pair
        return (
            remote(acc.at[slot], from_low.at[pair], r_send.at[0, pair], r_recv.at[0, pair], above),
            remote(acc.at[slot + 1], from_high.at[pair], r_send.at[1, pair], r_recv.at[1, pair], below),
        )

    flat = stage.reshape(4 * PARTS, SUBS * HELD, LANES)

    @pl.loop(0, 4)
    def _(pair):
        columns = [slot_column(pair, half, wave_pos) for half in range(2)]
        spots = []
        for end in range(2):
            low, high = [electrodes[pairs[column, end]] for column in columns]
            spots.append(jnp.where(sub < per_group, low, high) - tile_pos * ROWS + CORE)
        for copy in halo_copies(pair):
            copy.wait_recv()

        @pl.loop(FIRST, LAST)
        def _(row):
            for part in range(PARTS):
                rows8 = pl.ds(part * SUBS, SUBS)
                given = flat[pair * PARTS + part, pl.ds(row - FIRST, SUBS, HELD), :]
                w[0, row, rows8, :] = given * root[row, rows8, :]
            spot = jnp.where(row == spots[0], CURRENT, 0.0) - jnp.where(row == spots[1], CURRENT, 0.0)
            spot = (2.0 / DELTA) * spot * inverse[row, pl.ds(0, SUBS), :]
            src[row] = jnp.where(first_lane, spot, 0.0)

        for step in range(ITERS):
            sweep(step)

        @pl.loop(0, ROWS)
        def _(row):
            for part in range(PARTS):
                rows8 = pl.ds(part * SUBS, SUBS)
                zbuf[part, pl.ds(row, SUBS, ROWS), :] = (final * inverse[CORE + row, rows8, :]) * w[
                    ITERS % 2, CORE + row, rows8, :]

        for half in range(2):
            for part in range(PARTS):
                for row in range(0, ROWS, SUBS):
                    terms = [zbuf[part, pl.ds((half * per_group + k) * ROWS + row, SUBS), :] for k in range(per_group)]
                    acc[2 * pair + half, part, pl.ds(row, SUBS), :] = (terms[0] + terms[1]) + (terms[2] + terms[3])

        @pl.when(pair == 1)
        def _():
            rs_copies(0)[0].wait_recv()
            acc[2] += from_low[0]

        @pl.when(pair == 2)
        def _():
            rs_copies(0)[1].wait_recv()
            acc[5] += from_high[0]

        @pl.when(pair < 3)
        def _():
            for copy in rs_copies(pair):
                copy.start()

    for pair in (1, 2):
        for copy in rs_copies(pair):
            copy.wait_recv()
    total = jnp.concatenate([
        jnp.concatenate([acc[6 + half, part] + (from_low[1 + half, part] + from_high[1 + half, part])
                         for part in range(PARTS)], axis=1)
        for half in range(2)], axis=0)
    moved = jnp.dot(jnp.concatenate(thirds(total), axis=0), back[...], preferred_element_type=F32)
    for half in range(2):
        cut = half * ROWS
        out[half] = (moved[cut:cut + ROWS] + moved[2 * ROWS + cut:3 * ROWS + cut]) + moved[
            4 * ROWS + cut:5 * ROWS + cut]

    for pair in range(3):
        for copy in rs_copies(pair):
            copy.wait_send()
    for pair in range(4):
        for copy in halo_copies(pair):
            copy.wait_send()
    sig_south.wait_send()
    sig_north.wait_send()


def local(*arrays):
    fields = arrays[0]
    per_group, sources, rows, depth = fields.shape
    small = [pltpu.SMEM(a.shape, a.dtype) for a in arrays[2:]]
    tall = pltpu.VMEM((SPAN, PARTS * SUBS, LANES), F32)
    flat = pltpu.VMEM((PARTS, SPAN, LANES), F32)
    return pl.pallas_call(
        kernel,
        out_shape=jax.ShapeDtypeStruct((sources // 4, rows, depth), F32),
        in_specs=[pl.BlockSpec(memory_space=pl.ANY)] * len(arrays),
        out_specs=pl.BlockSpec(memory_space=pltpu.VMEM),
        scratch_shapes=[
            pltpu.VMEM(fields.shape, fields.dtype),
            pltpu.VMEM((rows, depth), F32),
            *small,
            pltpu.VMEM((depth, depth), BF16),
            pltpu.VMEM((depth, depth), BF16),
            pltpu.VMEM((4, PARTS, SUBS, HELD, LANES), F32),
            pltpu.VMEM((HALO, depth), F32),
            pltpu.VMEM((HALO, depth), F32),
            flat, flat, flat, flat,
            tall, tall, tall, tall,
            pltpu.VMEM((3 * ITERS, SUBS, LANES), F32),
            pltpu.VMEM((SPAN, SUBS, LANES), F32),
            pltpu.VMEM((2, SPAN, PARTS * SUBS, LANES), F32),
            pltpu.VMEM((PARTS, SUBS * ROWS, LANES), F32),
            pltpu.VMEM((sources, PARTS, rows, LANES), F32),
            pltpu.VMEM((3, PARTS, rows, LANES), F32),
            pltpu.VMEM((3, PARTS, rows, LANES), F32),
            pltpu.SemaphoreType.DMA((7,)),
            pltpu.SemaphoreType.DMA((2, 4)),
            pltpu.SemaphoreType.DMA((2, 4)),
            pltpu.SemaphoreType.DMA((2,)),
            pltpu.SemaphoreType.DMA((2,)),
            pltpu.SemaphoreType.DMA((2, 3)),
            pltpu.SemaphoreType.DMA((2, 3)),
        ],
        compiler_params=pltpu.CompilerParams(
            collective_id=0, has_side_effects=True, vmem_limit_bytes=48 * 1024 * 1024),
    )(*arrays)


def solution(mesh):
    placed = (P("wave", None, "tile", None), P("tile", None), P(), P(), P(), P(), P())
    return jax.shard_map(
        local, mesh=mesh, in_specs=placed, out_specs=P("wave", "tile", None), check_vma=False
    )
```

time: 507 us -> 59.6 us (0.12)
  starting transfers between devices: 261 us -> 0 us
  other arithmetic: 106 us -> 0 us
  waiting for transfers between devices: 53.6 us -> 0 us
  Pallas kernels: 0 us -> 52.8 us
  local copies, waits for them, and re-layouts: 38.5 us -> 6.57 us
  loops' own time: 30.6 us -> 0 us
  between operations: 13.4 us -> 0.02 us
    ppermute x66 -> x0, starting transfers between devices: 261 us -> none  [the longest x33 218 us: with_halo(): lax.ppermute(lax.slice_in_dim(block, block.shape[dim] - width, None, axis...]
    select_n x96 -> x0, other arithmetic: 81.7 us -> none  [the longest x32 67.1 us: chebyshev_step(): jnp.where(active, moved, direction)]
    reduce_scatter x1 -> x0, waiting for transfers between devices: 53.4 us -> none  [local(): return lax.psum_scatter(summed, 'wave', scatter_dimension=0, tiled=True)]
    pallas_call x0 -> x1, Pallas kernels: none -> 52.8 us  [local(): pl.pallas_call(kernel, out_shape=jax.ShapeDtypeStruct((sources // 4, rows...]
    another operation x5 -> x0, loops' own time: 30.6 us -> none  [the longest x4 24.6 us: advance(): lax.fori_loop(0, ITERS, sweep, (start, jnp.zeros_like(start), rho_start))[0]]
    slice x34 -> x0, local copies, waits for them, and re-layouts: 22.2 us -> none  [the longest x33 22.2 us: with_halo(): lax.slice_in_dim(block, block.shape[dim] - width, None, axis=dim)]
    add x10 -> x0, other arithmetic: 17.1 us -> none  [the longest x4 11.3 us: per_wave(): return (total + weight * solved, None)]
    dynamic_slice x15 -> x0, local copies, waits for them, and re-layouts: 16.1 us -> none  [the longest x12 12.9 us: local(): lax.scan(per_wave, jnp.zeros((source_count, row_count, col_count), jnp.fl...]
  transfers between devices with their start and end apart: 67 -> 0, of which waited for: 1 -> 0; matrix products, arithmetic and copies ran while one was open for 1% -> 0% of each run, Pallas kernels for 0% -> 0%
where the time goes in v2:
time: 59.6 us; the launch traced here: 59.3 us
  Pallas kernels  52.8 us (89%)
  local copies, waits for them, and re-layouts  6.57 us (11%)
    pallas_call x1, Pallas kernels, local(): pl.pallas_call(kernel, out_shape=jax.ShapeDtypeStruct((sources // 4, rows...  52.8 us
    unnamed x14, local copies, waits for them, and re-layouts  6.57 us

profile of v2, /device:TPU:0, one launch (start us, length us, event | category | flops | bytes accessed | tf_op | source)
XLA Modules:
  0.0 59.3 jit_solution(2258449914505267757)
XLA Ops:
  0.0 0.8 %copy.8.pairs_in = s32[8,2]{1,0:T(8,128)S(1)} copy(s32[8,2]{0,1:T(2,128)} %param.13) | data formatting | bytes 128 | tf_op args[6]
  0.8 0.0 copy-start
  0.8 1.6 %copy-done = bf16[4,8,32,1024]{3,2,1,0:T(8,128)(2,1)S(1)} copy-done((bf16[4,8,32,1024]{3,2,1,0:T(8,128)(2,1)S(1)}, bf16[4,8,32,1024]{3,2,1,0:T(8,128)(2,1)}, u32[]{:S(2)}) %copy-start) | copy-done | bytes 2097176
  2.3 0.0 copy-start.1
  2.3 0.9 %copy-done.1 = f32[32,1024]{1,0:T(8,128)S(1)} copy-done((f32[32,1024]{1,0:T(8,128)S(1)}, f32[32,1024]{1,0:T(8,128)}, u32[]{:S(2)}) %copy-start.1) | copy-done | bytes 131096
  3.2 0.0 copy-start.2
  3.3 0.7 %copy-done.2 = f32[16]{0:T(128)S(1)} copy-done((f32[16]{0:T(128)S(1)}, f32[16]{0:T(128)}, u32[]{:S(2)}) %copy-start.2) | copy-done | bytes 88
  3.9 0.0 copy-start.3
  3.9 0.7 %copy-done.3 = f32[16]{0:T(128)S(1)} copy-done((f32[16]{0:T(128)S(1)}, f32[16]{0:T(128)}, u32[]{:S(2)}) %copy-start.3) | copy-done | bytes 88
  4.6 0.0 copy-start.4
  4.6 0.7 %copy-done.4 = s32[16]{0:T(128)S(1)} copy-done((s32[16]{0:T(128)S(1)}, s32[16]{0:T(128)}, u32[]{:S(2)}) %copy-start.4) | copy-done | bytes 88
  5.2 0.0 copy-start.5
  5.2 0.7 %copy-done.5 = s32[64]{0:T(128)S(1)} copy-done((s32[64]{0:T(128)S(1)}, s32[64]{0:T(128)}, u32[]{:S(2)}) %copy-start.5) | copy-done | bytes 280
  5.9 52.8 %shard_map.73 = f32[2,32,1024]{2,1,0:T(8,128)S(1)} custom-call(bf16[4,8,32,1024]{3,2,1,0:T(8,128)(2,1)S(1)} %copy-done, f32[32,1024]{1,0:T(8,128)S(1)} %copy-done.1, f32[16]{0:T(128)S(1)} %copy-done.2, f32[16]{0:T(128)S(1)} %copy-done.3, s32[16]{0:T(128)S(1)} %copy-done.4, s32[64]{0:T(128)S(1)} %copy-done.5, s32[8,2]{1,0:T(8,128)S(1)} %copy.8.pairs_in), custom_call_target="tpu_custom_call" | custom-call | tf_op jit(solution)/shard_map/pallas_call | solution.py:351
  58.6 0.7 %copy.10 = f32[2,32,1024]{2,1,0:T(8,128)} copy(f32[2,32,1024]{2,1,0:T(8,128)S(1)} %shard_map.73) | data formatting | bytes 524288
Async XLA Ops:
  0.8 1.6 %copy-start = (bf16[4,8,32,1024]{3,2,1,0:T(8,128)(2,1)S(1)}, bf16[4,8,32,1024]{3,2,1,0:T(8,128)(2,1)}, u32[]{:S(2)}) copy-start(bf16[4,8,32,1024]{3,2,1,0:T(8,128)(2,1)} %fields_in.1) | copy-start | bytes 6291460
  2.3 0.9 %copy-start.1 = (f32[32,1024]{1,0:T(8,128)S(1)}, f32[32,1024]{1,0:T(8,128)}, u32[]{:S(2)}) copy-start(f32[32,1024]{1,0:T(8,128)} %sigma_in.1) | copy-start | bytes 393220
  3.2 0.7 %copy-start.2 = (f32[16]{0:T(128)S(1)}, f32[16]{0:T(128)}, u32[]{:S(2)}) copy-start(f32[16]{0:T(128)} %wavenumbers_in.1) | copy-start | bytes 196
  3.9 0.7 %copy-start.3 = (f32[16]{0:T(128)S(1)}, f32[16]{0:T(128)}, u32[]{:S(2)}) copy-start(f32[16]{0:T(128)} %weights_in.1) | copy-start | bytes 196
  4.6 0.7 %copy-start.4 = (s32[16]{0:T(128)S(1)}, s32[16]{0:T(128)}, u32[]{:S(2)}) copy-start(s32[16]{0:T(128)} %counts_in.1) | copy-start | bytes 196
  5.2 0.7 %copy-start.5 = (s32[64]{0:T(128)S(1)}, s32[64]{0:T(128)}, u32[]{:S(2)}) copy-start(s32[64]{0:T(128)} %electrodes_in.1) | copy-start | bytes 772

commit v3 on v2

--- a/solution.py
+++ b/solution.py
@@ -28,7 +28,7 @@
 FIRST = 8
 CORE = FIRST + HALO
 LAST = FIRST + HELD
-UNROLL = 4
+UNROLL = ((8, 6), (9, 5), (11, 4), (7, 6), (8, 5), (8, 5), (7, 5), (11, 3))
 MESH = pl.DeviceIdType.MESH
 F32 = jnp.float32
 BF16 = jnp.bfloat16
@@ -59,8 +59,8 @@
 def kernel(
     fields_in, sigma_in, wavenumbers_in, weights_in, counts_in, electrodes_in, pairs_in, out,
     fields, sigma, wavenumbers, weights, counts, electrodes, pairs,
-    into, back, stage, sig_n, sig_s, sig, diag, face_n, face_w,
-    an, aw, root, inverse, vectors, src, w, zbuf, acc, from_low, from_high,
+    into, back, weave, stage, sig_n, sig_s, sig, diag, face_n, face_w,
+    an, aw, root, close, vectors, src, w, acc, from_low, from_high,
     in_sem, h_send, h_recv, s_send, s_recv, r_send, r_recv,
 ):
     per_group = fields.shape[0]
@@ -103,12 +103,17 @@
         back[pl.ds(base, LANES), :] = jnp.where(
             column == lax.rem(row, LANES) * PARTS + lax.div(row, LANES), 1.0, 0.0).astype(BF16)
 
+    row = lax.broadcasted_iota(jnp.int32, weave.shape, 0)
+    column = lax.broadcasted_iota(jnp.int32, weave.shape, 1)
+    weave[...] = jnp.where(
+        column == lax.rem(row, SUBS) * ROWS + lax.div(row, SUBS), 1.0, 0.0).astype(BF16)
+
     for part in range(PARTS):
         rows8 = pl.ds(part * SUBS, SUBS)
         for row in range(LAST, SPAN):
             an[row, rows8, :] = zero
             aw[row, rows8, :] = zero
-            src[row] = zero
+            src[0, row] = zero
             for buf in range(2):
                 w[buf, row, rows8, :] = zero
         for edge in (0, LAST):
@@ -131,9 +136,9 @@
 
     def halo_copies(pair):
         return (
-            remote(stage.at[pair, :, :, pl.ds(ROWS, HALO)], stage.at[pair, :, :, pl.ds(0, HALO)],
+            remote(stage.at[pair, pl.ds(ROWS, HALO)], stage.at[pair, pl.ds(0, HALO)],
                    h_send.at[0, pair], h_recv.at[0, pair], south),
-            remote(stage.at[pair, :, :, pl.ds(HALO, HALO)], stage.at[pair, :, :, pl.ds(HALO + ROWS, HALO)],
+            remote(stage.at[pair, pl.ds(HALO, HALO)], stage.at[pair, pl.ds(HALO + ROWS, HALO)],
                    h_send.at[1, pair], h_recv.at[1, pair], north),
         )
 
@@ -142,11 +147,12 @@
         columns = [slot_column(pair, half, wave_pos) for half in range(2)]
         block = jnp.concatenate(
             [fields[k, columns[half]] for half in range(2) for k in range(per_group)], axis=0)
-        moved = jnp.dot(block, into[...], preferred_element_type=F32)
-        for part in range(PARTS):
-            for place in range(SUBS):
-                stage[pair, part, place, pl.ds(HALO, ROWS), :] = moved[
-                    place * ROWS:(place + 1) * ROWS, part * LANES:(part + 1) * LANES]
+        woven = jnp.dot(weave[...], block, preferred_element_type=F32).astype(BF16)
+        moved = jnp.dot(woven, into[...], preferred_element_type=F32)
+        for row in range(ROWS):
+            for part in range(PARTS):
+                stage[pair, HALO + row, pl.ds(part * SUBS, SUBS), :] = moved[
+                    row * SUBS:(row + 1) * SUBS, part * LANES:(part + 1) * LANES]
         for copy in halo_copies(pair):
             copy.start()
 
@@ -214,9 +220,10 @@
             guess = lax.rsqrt(value)
             guess = guess * (1.5 - (0.5 * value) * (guess * guess))
             root[row, rows8, :] = value * guess
-            inverse[row, rows8, :] = guess
+            close[row, rows8, :] = final * guess
             an[row, rows8, :] = spread(face_n, part) * (guess * above_row[part])
             here.append(guess)
+        src[1, row] = here[0]
         for part in range(PARTS):
             beside = here[part - 1] if part else pltpu.roll(here[-1], 1, 1)
             aw[row, pl.ds(part * SUBS, SUBS), :] = spread(face_w, part) * (here[part] * beside)
@@ -231,29 +238,35 @@
         side_gain = vectors[3 * step + 1]
         charge = vectors[3 * step + 2]
         start = FIRST + step + 1
-        blocks = -(-(HELD - 1 - 2 * step) // UNROLL)
+        unroll, blocks = UNROLL[step]
         parts = [pl.ds(part * SUBS, SUBS) for part in range(PARTS)]
 
         def one(row, carry):
             old, sums = carry
-            u = [w[now, row, at, :] for at in parts]
-            north_c = [an[row, at, :] for at in parts]
-            west_c = [aw[row, at, :] for at in parts]
+            edge = pltpu.roll(w[now, row, parts[-1], :], 1, 1)
+            u, held, flow_first = [], [], None
             for part, at in enumerate(parts):
-                value = side_gain * (sums[part] + north_c[part] * u[part]) + (
+                here = w[now, row, at, :]
+                north_c = an[row, at, :]
+                value = side_gain * (sums[part] + north_c * here) + (
                     centre_gain * old[part] - w[before, row - 1, at, :])
                 if part == 0:
-                    value = value + charge * src[row - 1]
+                    value = value + charge * src[0, row - 1]
                 w[later, row - 1, at, :] = value
-            flows = [west_c[part] * u[part] for part in range(PARTS)]
-            left = [pltpu.roll(u[-1], 1, 1)] + u[:-1]
-            right = flows[1:] + [pltpu.roll(flows[0], LANES - 1, 1)]
-            sums = [north_c[part] * old[part] + (west_c[part] * left[part] + right[part]) for part in range(PARTS)]
-            return tuple(u), tuple(sums)
+                west_c = aw[row, at, :]
+                flow = west_c * here
+                if part == 0:
+                    flow_first = pltpu.roll(flow, LANES - 1, 1)
+                else:
+                    held[-1] = held[-1] + flow
+                held.append(north_c * old[part] + west_c * (u[-1] if part else edge))
+                u.append(here)
+            held[-1] = held[-1] + flow_first
+            return tuple(u), tuple(held)
 
         def body(block, carry):
-            for place in range(UNROLL):
-                carry = one(start + UNROLL * block + place, carry)
+            for place in range(unroll):
+                carry = one(start + unroll * block + place, carry)
             return carry
 
         opening = tuple(w[now, start - 1, at, :] for at in parts)
@@ -266,14 +279,12 @@
             remote(acc.at[slot + 1], from_high.at[pair], r_send.at[1, pair], r_recv.at[1, pair], below),
         )
 
-    flat = stage.reshape(4 * PARTS, SUBS * HELD, LANES)
-
     @pl.loop(0, 4)
     def _(pair):
         columns = [slot_column(pair, half, wave_pos) for half in range(2)]
         spots = []
         for end in range(2):
-            low, high = [electrodes[pairs[column, end]] for column in columns]
+            low, high = [electrodes[pairs[end, column]] for column in columns]
             spots.append(jnp.where(sub < per_group, low, high) - tile_pos * ROWS + CORE)
         for copy in halo_copies(pair):
             copy.wait_recv()
@@ -282,11 +293,10 @@
         def _(row):
             for part in range(PARTS):
                 rows8 = pl.ds(part * SUBS, SUBS)
-                given = flat[pair * PARTS + part, pl.ds(row - FIRST, SUBS, HELD), :]
-                w[0, row, rows8, :] = given * root[row, rows8, :]
+                w[0, row, rows8, :] = stage[pair, row - FIRST, rows8, :] * root[row, rows8, :]
             spot = jnp.where(row == spots[0], CURRENT, 0.0) - jnp.where(row == spots[1], CURRENT, 0.0)
-            spot = (2.0 / DELTA) * spot * inverse[row, pl.ds(0, SUBS), :]
-            src[row] = jnp.where(first_lane, spot, 0.0)
+            spot = (2.0 / DELTA) * spot * src[1, row]
+            src[0, row] = jnp.where(first_lane, spot, 0.0)
 
         for step in range(ITERS):
             sweep(step)
@@ -295,14 +305,11 @@
         def _(row):
             for part in range(PARTS):
                 rows8 = pl.ds(part * SUBS, SUBS)
-                zbuf[part, pl.ds(row, SUBS, ROWS), :] = (final * inverse[CORE + row, rows8, :]) * w[
-                    ITERS % 2, CORE + row, rows8, :]
-
-        for half in range(2):
-            for part in range(PARTS):
-                for row in range(0, ROWS, SUBS):
-                    terms = [zbuf[part, pl.ds((half * per_group + k) * ROWS + row, SUBS), :] for k in range(per_group)]
-                    acc[2 * pair + half, part, pl.ds(row, SUBS), :] = (terms[0] + terms[1]) + (terms[2] + terms[3])
+                value = close[CORE + row, rows8, :] * w[ITERS % 2, CORE + row, rows8, :]
+                value = value + pltpu.roll(value, SUBS - 2, 0)
+                value = value + pltpu.roll(value, SUBS - 1, 0)
+                for half in range(2):
+                    acc[2 * pair + half, part, pl.ds(row, 1), :] = value[half * per_group:half * per_group + 1]
 
         @pl.when(pair == 1)
         def _():
@@ -343,6 +350,7 @@
 
 
 def local(*arrays):
+    arrays = (*arrays[:-1], arrays[-1].T)
     fields = arrays[0]
     per_group, sources, rows, depth = fields.shape
     small = [pltpu.SMEM(a.shape, a.dtype) for a in arrays[2:]]
@@ -351,7 +359,7 @@
     return pl.pallas_call(
         kernel,
         out_shape=jax.ShapeDtypeStruct((sources // 4, rows, depth), F32),
-        in_specs=[pl.BlockSpec(memory_space=pl.ANY)] * len(arrays),
+        in_specs=[pl.BlockSpec(memory_space=pltpu.HBM)] * len(arrays),
         out_specs=pl.BlockSpec(memory_space=pltpu.VMEM),
         scratch_shapes=[
             pltpu.VMEM(fields.shape, fields.dtype),
@@ -359,15 +367,15 @@
             *small,
             pltpu.VMEM((depth, depth), BF16),
             pltpu.VMEM((depth, depth), BF16),
-            pltpu.VMEM((4, PARTS, SUBS, HELD, LANES), F32),
+            pltpu.VMEM((SUBS * rows, SUBS * rows), BF16),
+            pltpu.VMEM((4, HELD, PARTS * SUBS, LANES), F32),
             pltpu.VMEM((HALO, depth), F32),
             pltpu.VMEM((HALO, depth), F32),
             flat, flat, flat, flat,
             tall, tall, tall, tall,
             pltpu.VMEM((3 * ITERS, SUBS, LANES), F32),
-            pltpu.VMEM((SPAN, SUBS, LANES), F32),
+            pltpu.VMEM((2, SPAN, SUBS, LANES), F32),
             pltpu.VMEM((2, SPAN, PARTS * SUBS, LANES), F32),
-            pltpu.VMEM((PARTS, SUBS * ROWS, LANES), F32),
             pltpu.VMEM((sources, PARTS, rows, LANES), F32),
             pltpu.VMEM((3, PARTS, rows, LANES), F32),
             pltpu.VMEM((3, PARTS, rows, LANES), F32),
@@ -380,7 +388,7 @@
             pltpu.SemaphoreType.DMA((2, 3)),
         ],
         compiler_params=pltpu.CompilerParams(
-            collective_id=0, has_side_effects=True, vmem_limit_bytes=48 * 1024 * 1024),
+            collective_id=0, has_side_effects=True, vmem_limit_bytes=63 * 1024 * 1024),
     )(*arrays)
 
 

time: 59.6 us -> 41.9 us (0.70)
  Pallas kernels: 52.8 us -> 40.1 us
  local copies, waits for them, and re-layouts: 6.57 us -> 1.67 us
    pallas_call x1, Pallas kernels: 52.8 us -> 40.1 us  [local(): pl.pallas_call(kernel, out_shape=jax.ShapeDtypeStruct((sources // 4, rows...]
    unnamed x14 -> x1, local copies, waits for them, and re-layouts: 6.57 us -> 1.67 us
where the time goes in v3:
time: 41.9 us; the launch traced here: 41.7 us
  Pallas kernels  40.1 us (96%)
  local copies, waits for them, and re-layouts  1.67 us (4%)
    pallas_call x1, Pallas kernels, local(): pl.pallas_call(kernel, out_shape=jax.ShapeDtypeStruct((sources // 4, rows...  40.1 us
    unnamed x1, local copies, waits for them, and re-layouts  1.67 us

profile of v3, /device:TPU:0, one launch (start us, length us, event | category | flops | bytes accessed | tf_op | source)
XLA Modules:
  0.0 41.7 jit_solution(9770135393738087198)
XLA Ops:
  0.0 40.1 %shard_map.73 = f32[2,32,1024]{2,1,0:T(8,128)} custom-call(bf16[4,8,32,1024]{3,2,1,0:T(8,128)(2,1)} %fields_in.1, f32[32,1024]{1,0:T(8,128)} %sigma_in.1, f32[16]{0:T(128)} %wavenumbers_in.1, f32[16]{0:T(128)} %weights_in.1, s32[16]{0:T(128)} %counts_in.1, s32[64]{0:T(128)} %electrodes_in.1, s32[2,8]{1,0:T(2,128)} %bitcast.1), custom_call_target="tpu_custom_call" | custom-call | tf_op jit(solution)/shard_map/pallas_call | solution.py:359
  40.1 1.7 %copy.9 = f32[2,32,1024]{2,1,0:T(8,128)} copy(f32[2,32,1024]{2,1,0:T(8,128)} %shard_map.73) | data formatting | bytes 524288

commit v4 on v3

--- a/solution.py
+++ b/solution.py
@@ -136,31 +136,35 @@
 
     def halo_copies(pair):
         return (
-            remote(stage.at[pair, pl.ds(ROWS, HALO)], stage.at[pair, pl.ds(0, HALO)],
+            remote(stage.at[pair, pl.ds(ROWS * SUBS, HALO * SUBS)], stage.at[pair, pl.ds(0, HALO * SUBS)],
                    h_send.at[0, pair], h_recv.at[0, pair], south),
-            remote(stage.at[pair, pl.ds(HALO, HALO)], stage.at[pair, pl.ds(HALO + ROWS, HALO)],
+            remote(stage.at[pair, pl.ds(HALO * SUBS, HALO * SUBS)],
+                   stage.at[pair, pl.ds((HALO + ROWS) * SUBS, HALO * SUBS)],
                    h_send.at[1, pair], h_recv.at[1, pair], north),
         )
 
-    @pl.loop(0, 4)
-    def _(pair):
-        columns = [slot_column(pair, half, wave_pos) for half in range(2)]
-        block = jnp.concatenate(
-            [fields[k, columns[half]] for half in range(2) for k in range(per_group)], axis=0)
-        woven = jnp.dot(weave[...], block, preferred_element_type=F32).astype(BF16)
-        moved = jnp.dot(woven, into[...], preferred_element_type=F32)
-        for row in range(ROWS):
-            for part in range(PARTS):
-                stage[pair, HALO + row, pl.ds(part * SUBS, SUBS), :] = moved[
-                    row * SUBS:(row + 1) * SUBS, part * LANES:(part + 1) * LANES]
-        for copy in halo_copies(pair):
-            copy.start()
+    @pl.loop(0, 2)
+    def _(batch):
+        woven = []
+        for pair in (2 * batch, 2 * batch + 1):
+            columns = [slot_column(pair, half, wave_pos) for half in range(2)]
+            block = jnp.concatenate(
+                [fields[k, columns[half]] for half in range(2) for k in range(per_group)], axis=0)
+            woven.append(jnp.dot(weave[...], block, preferred_element_type=F32).astype(BF16))
+        moved = jnp.dot(jnp.concatenate(woven, axis=0), into[...], preferred_element_type=F32).astype(BF16)
+        for place, pair in enumerate((2 * batch, 2 * batch + 1)):
+            stage[pair, pl.ds(HALO * SUBS, ROWS * SUBS), :] = moved[place * ROWS * SUBS:(place + 1) * ROWS * SUBS]
+            for copy in halo_copies(pair):
+                copy.start()
 
     def by_wavenumber(scalars):
         value = zero
         for k, scalar in enumerate(scalars):
             value = jnp.where(lax.rem(sub, per_group) == k, scalar, value)
         return value
+
+    def everywhere(scalars):
+        return jnp.concatenate([by_wavenumber(scalars)] * PARTS, axis=0)
 
     group = [wave_pos * per_group + k for k in range(per_group)]
     square = by_wavenumber([wavenumbers[g] * wavenumbers[g] for g in group])
@@ -168,11 +172,11 @@
         weights[g] * chosen(counts[g], [1.0 / tau for tau in TAU[: ITERS + 1]]) for g in group])
     for step in range(ITERS):
         live = [step - (ITERS - counts[g]) for g in group]
-        vectors[3 * step] = by_wavenumber([
+        vectors[3 * step] = everywhere([
             jnp.where(at < 0, F32(2.0), jnp.where(at == 0, F32(1.0 + 0.5 * OMEGA), F32(OMEGA))) for at in live])
-        vectors[3 * step + 1] = by_wavenumber([
+        vectors[3 * step + 1] = everywhere([
             jnp.where(at < 0, F32(0.0), jnp.where(at == 0, F32(0.5), F32(1.0))) for at in live])
-        vectors[3 * step + 2] = by_wavenumber([chosen(at, [0.5] + TAU[1:ITERS]) for at in live])
+        vectors[3 * step + 2] = everywhere([chosen(at, [0.5] + TAU[1:ITERS]) for at in live])
 
     sig_south.wait_recv()
     sig_north.wait_recv()
@@ -229,14 +233,15 @@
             aw[row, pl.ds(part * SUBS, SUBS), :] = spread(face_w, part) * (here[part] * beside)
         return tuple(here)
 
-    lax.fori_loop(FIRST, LAST, couplings, (zero,) * PARTS)
+    def two_rows(block, above_row):
+        return couplings(FIRST + 2 * block + 1, couplings(FIRST + 2 * block, above_row))
+
+    lax.fori_loop(0, HELD // 2, two_rows, (zero,) * PARTS)
 
     def sweep(step):
         now, later = step % 2, (step + 1) % 2
         before = now if step == 0 else later
-        centre_gain = vectors[3 * step]
-        side_gain = vectors[3 * step + 1]
-        charge = vectors[3 * step + 2]
+        charge = vectors[3 * step + 2, pl.ds(0, SUBS), :]
         start = FIRST + step + 1
         unroll, blocks = UNROLL[step]
         parts = [pl.ds(part * SUBS, SUBS) for part in range(PARTS)]
@@ -248,6 +253,7 @@
             for part, at in enumerate(parts):
                 here = w[now, row, at, :]
                 north_c = an[row, at, :]
+                side_gain, centre_gain = vectors[3 * step + 1, at, :], vectors[3 * step, at, :]
                 value = side_gain * (sums[part] + north_c * here) + (
                     centre_gain * old[part] - w[before, row - 1, at, :])
                 if part == 0:
@@ -289,27 +295,34 @@
         for copy in halo_copies(pair):
             copy.wait_recv()
 
-        @pl.loop(FIRST, LAST)
-        def _(row):
-            for part in range(PARTS):
-                rows8 = pl.ds(part * SUBS, SUBS)
-                w[0, row, rows8, :] = stage[pair, row - FIRST, rows8, :] * root[row, rows8, :]
-            spot = jnp.where(row == spots[0], CURRENT, 0.0) - jnp.where(row == spots[1], CURRENT, 0.0)
-            spot = (2.0 / DELTA) * spot * src[1, row]
-            src[0, row] = jnp.where(first_lane, spot, 0.0)
+        @pl.loop(0, HELD // 4)
+        def _(block):
+            for twin in (2 * block, 2 * block + 1):
+                for part in range(PARTS):
+                    rows8 = pl.ds(part * SUBS, SUBS)
+                    given = stage[pair, pl.ds(twin * 2 * SUBS, 2 * SUBS), pl.ds(part * LANES, LANES)].astype(F32)
+                    for place in range(2):
+                        row = FIRST + 2 * twin + place
+                        w[0, row, rows8, :] = given[place * SUBS:(place + 1) * SUBS] * root[row, rows8, :]
+            for place in range(4):
+                row = FIRST + 4 * block + place
+                spot = jnp.where(row == spots[0], CURRENT, 0.0) - jnp.where(row == spots[1], CURRENT, 0.0)
+                spot = (2.0 / DELTA) * spot * src[1, row]
+                src[0, row] = jnp.where(first_lane, spot, 0.0)
 
         for step in range(ITERS):
             sweep(step)
 
-        @pl.loop(0, ROWS)
-        def _(row):
-            for part in range(PARTS):
-                rows8 = pl.ds(part * SUBS, SUBS)
-                value = close[CORE + row, rows8, :] * w[ITERS % 2, CORE + row, rows8, :]
-                value = value + pltpu.roll(value, SUBS - 2, 0)
-                value = value + pltpu.roll(value, SUBS - 1, 0)
-                for half in range(2):
-                    acc[2 * pair + half, part, pl.ds(row, 1), :] = value[half * per_group:half * per_group + 1]
+        @pl.loop(0, ROWS // 4)
+        def _(block):
+            for row in [4 * block + place for place in range(4)]:
+                for part in range(PARTS):
+                    rows8 = pl.ds(part * SUBS, SUBS)
+                    value = close[CORE + row, rows8, :] * w[ITERS % 2, CORE + row, rows8, :]
+                    value = value + pltpu.roll(value, SUBS - 2, 0)
+                    value = value + pltpu.roll(value, SUBS - 1, 0)
+                    for half in range(2):
+                        acc[2 * pair + half, part, pl.ds(row, 1), :] = value[half * per_group:half * per_group + 1]
 
         @pl.when(pair == 1)
         def _():
@@ -368,12 +381,12 @@
             pltpu.VMEM((depth, depth), BF16),
             pltpu.VMEM((depth, depth), BF16),
             pltpu.VMEM((SUBS * rows, SUBS * rows), BF16),
-            pltpu.VMEM((4, HELD, PARTS * SUBS, LANES), F32),
+            pltpu.VMEM((4, HELD * SUBS, depth), BF16),
             pltpu.VMEM((HALO, depth), F32),
             pltpu.VMEM((HALO, depth), F32),
             flat, flat, flat, flat,
             tall, tall, tall, tall,
-            pltpu.VMEM((3 * ITERS, SUBS, LANES), F32),
+            pltpu.VMEM((3 * ITERS, PARTS * SUBS, LANES), F32),
             pltpu.VMEM((2, SPAN, SUBS, LANES), F32),
             pltpu.VMEM((2, SPAN, PARTS * SUBS, LANES), F32),
             pltpu.VMEM((sources, PARTS, rows, LANES), F32),

time: 41.9 us -> 37.1 us (0.89)
  Pallas kernels: 40.1 us -> 35.3 us
    pallas_call x1, Pallas kernels: 40.1 us -> 35.3 us  [local(): pl.pallas_call(kernel, out_shape=jax.ShapeDtypeStruct((sources // 4, rows...]
where the time goes in v4:
time: 37.1 us; the launch traced here: 37 us
  Pallas kernels  35.3 us (95%)
  local copies, waits for them, and re-layouts  1.67 us (5%)
    pallas_call x1, Pallas kernels, local(): pl.pallas_call(kernel, out_shape=jax.ShapeDtypeStruct((sources // 4, rows...  35.3 us
    unnamed x1, local copies, waits for them, and re-layouts  1.67 us

profile of v4, /device:TPU:0, one launch (start us, length us, event | category | flops | bytes accessed | tf_op | source)
XLA Modules:
  0.0 37.0 jit_solution(4201421538459171795)
XLA Ops:
  0.0 35.3 %shard_map.73 = f32[2,32,1024]{2,1,0:T(8,128)} custom-call(bf16[4,8,32,1024]{3,2,1,0:T(8,128)(2,1)} %fields_in.1, f32[32,1024]{1,0:T(8,128)} %sigma_in.1, f32[16]{0:T(128)} %wavenumbers_in.1, f32[16]{0:T(128)} %weights_in.1, s32[16]{0:T(128)} %counts_in.1, s32[64]{0:T(128)} %electrodes_in.1, s32[2,8]{1,0:T(2,128)} %bitcast.1), custom_call_target="tpu_custom_call" | custom-call | tf_op jit(solution)/shard_map/pallas_call | solution.py:372
  35.3 1.7 %copy.9 = f32[2,32,1024]{2,1,0:T(8,128)} copy(f32[2,32,1024]{2,1,0:T(8,128)} %shard_map.73) | data formatting | bytes 524288

commit v5 on v4

--- a/solution.py
+++ b/solution.py
@@ -77,14 +77,24 @@
     for other in (south, north, above, below):
         pl.semaphore_signal(barrier, inc=1, device_id=other, device_id_type=MESH)
 
+    def remote(source, target, send, recv, device):
+        return pltpu.make_async_remote_copy(
+            src_ref=source, dst_ref=target, send_sem=send, recv_sem=recv,
+            device_id=device, device_id_type=MESH,
+        )
+
+    sources = [(fields_in.at[k], fields.at[k]) for k in range(per_group)] + [
+        (sigma_in, sigma), (wavenumbers_in, wavenumbers), (weights_in, weights),
+        (counts_in, counts), (electrodes_in, electrodes), (pairs_in, pairs)]
     loads = [
-        pltpu.make_async_copy(source, target, in_sem.at[place])
-        for place, (source, target) in enumerate((
-            (fields_in, fields), (sigma_in, sigma), (wavenumbers_in, wavenumbers), (weights_in, weights),
-            (counts_in, counts), (electrodes_in, electrodes), (pairs_in, pairs)))
-    ]
+        pltpu.make_async_copy(source, target, in_sem.at[place]) for place, (source, target) in enumerate(sources)]
     for load in loads:
         load.start()
+    sig_south = remote(sigma_in.at[pl.ds(ROWS - HALO, HALO)], sig_n, s_send.at[0], s_recv.at[0], south)
+    sig_north = remote(sigma_in.at[pl.ds(0, HALO)], sig_s, s_send.at[1], s_recv.at[1], north)
+    pl.semaphore_wait(barrier, 4)
+    sig_south.start()
+    sig_north.start()
 
     lane = lax.broadcasted_iota(jnp.int32, (SUBS, LANES), 1)
     sub = lax.broadcasted_iota(jnp.int32, (SUBS, LANES), 0)
@@ -121,19 +131,6 @@
 
     for load in loads:
         load.wait()
-    pl.semaphore_wait(barrier, 4)
-
-    def remote(source, target, send, recv, device):
-        return pltpu.make_async_remote_copy(
-            src_ref=source, dst_ref=target, send_sem=send, recv_sem=recv,
-            device_id=device, device_id_type=MESH,
-        )
-
-    sig_south = remote(sigma.at[pl.ds(ROWS - HALO, HALO)], sig_n, s_send.at[0], s_recv.at[0], south)
-    sig_north = remote(sigma.at[pl.ds(0, HALO)], sig_s, s_send.at[1], s_recv.at[1], north)
-    sig_south.start()
-    sig_north.start()
-
     def halo_copies(pair):
         return (
             remote(stage.at[pair, pl.ds(ROWS * SUBS, HALO * SUBS)], stage.at[pair, pl.ds(0, HALO * SUBS)],
@@ -222,7 +219,6 @@
             rows8 = pl.ds(part * SUBS, SUBS)
             value = spread(diag, part) + square * spread(sig, part)
             guess = lax.rsqrt(value)
-            guess = guess * (1.5 - (0.5 * value) * (guess * guess))
             root[row, rows8, :] = value * guess
             close[row, rows8, :] = final * guess
             an[row, rows8, :] = spread(face_n, part) * (guess * above_row[part])
@@ -233,10 +229,12 @@
             aw[row, pl.ds(part * SUBS, SUBS), :] = spread(face_w, part) * (here[part] * beside)
         return tuple(here)
 
-    def two_rows(block, above_row):
-        return couplings(FIRST + 2 * block + 1, couplings(FIRST + 2 * block, above_row))
-
-    lax.fori_loop(0, HELD // 2, two_rows, (zero,) * PARTS)
+    def four_rows(block, above_row):
+        for place in range(4):
+            above_row = couplings(FIRST + 4 * block + place, above_row)
+        return above_row
+
+    lax.fori_loop(0, HELD // 4, four_rows, (zero,) * PARTS)
 
     def sweep(step):
         now, later = step % 2, (step + 1) % 2
@@ -392,7 +390,7 @@
             pltpu.VMEM((sources, PARTS, rows, LANES), F32),
             pltpu.VMEM((3, PARTS, rows, LANES), F32),
             pltpu.VMEM((3, PARTS, rows, LANES), F32),
-            pltpu.SemaphoreType.DMA((7,)),
+            pltpu.SemaphoreType.DMA((10,)),
             pltpu.SemaphoreType.DMA((2, 4)),
             pltpu.SemaphoreType.DMA((2, 4)),
             pltpu.SemaphoreType.DMA((2,)),

time: 37.1 us -> 37.8 us (1.019)
  Pallas kernels: 35.3 us -> 36 us
    pallas_call x1, Pallas kernels: 35.3 us -> 36 us  [local(): pl.pallas_call(kernel, out_shape=jax.ShapeDtypeStruct((sources // 4, rows...]
where the time goes in v5:
time: 37.8 us; the launch traced here: 37.7 us
  Pallas kernels  36 us (95%)
  local copies, waits for them, and re-layouts  1.67 us (4%)
    pallas_call x1, Pallas kernels, local(): pl.pallas_call(kernel, out_shape=jax.ShapeDtypeStruct((sources // 4, rows...  36 us
    unnamed x1, local copies, waits for them, and re-layouts  1.67 us

profile of v5, /device:TPU:0, one launch (start us, length us, event | category | flops | bytes accessed | tf_op | source)
XLA Modules:
  0.0 37.7 jit_solution(6929719170297169217)
XLA Ops:
  0.0 36.0 %shard_map.73 = f32[2,32,1024]{2,1,0:T(8,128)} custom-call(bf16[4,8,32,1024]{3,2,1,0:T(8,128)(2,1)} %fields_in.1, f32[32,1024]{1,0:T(8,128)} %sigma_in.1, f32[16]{0:T(128)} %wavenumbers_in.1, f32[16]{0:T(128)} %weights_in.1, s32[16]{0:T(128)} %counts_in.1, s32[64]{0:T(128)} %electrodes_in.1, s32[2,8]{1,0:T(2,128)} %bitcast.1), custom_call_target="tpu_custom_call" | custom-call | tf_op jit(solution)/shard_map/pallas_call | solution.py:370
  36.0 1.7 %copy.9 = f32[2,32,1024]{2,1,0:T(8,128)} copy(f32[2,32,1024]{2,1,0:T(8,128)} %shard_map.73) | data formatting | bytes 524288

commit v6 on v5

--- a/solution.py
+++ b/solution.py
@@ -92,9 +92,6 @@
         load.start()
     sig_south = remote(sigma_in.at[pl.ds(ROWS - HALO, HALO)], sig_n, s_send.at[0], s_recv.at[0], south)
     sig_north = remote(sigma_in.at[pl.ds(0, HALO)], sig_s, s_send.at[1], s_recv.at[1], north)
-    pl.semaphore_wait(barrier, 4)
-    sig_south.start()
-    sig_north.start()
 
     lane = lax.broadcasted_iota(jnp.int32, (SUBS, LANES), 1)
     sub = lax.broadcasted_iota(jnp.int32, (SUBS, LANES), 0)
@@ -128,6 +125,10 @@
                 w[buf, row, rows8, :] = zero
         for edge in (0, LAST):
             sig[part, pl.ds(edge, FIRST), :] = zero + 1.0
+
+    pl.semaphore_wait(barrier, 4)
+    sig_south.start()
+    sig_north.start()
 
     for load in loads:
         load.wait()

time: 37.8 us -> 36.7 us (0.971)
  Pallas kernels: 36 us -> 34.9 us
    pallas_call x1, Pallas kernels: 36 us -> 34.9 us  [local(): pl.pallas_call(kernel, out_shape=jax.ShapeDtypeStruct((sources // 4, rows...]
where the time goes in v6:
time: 36.7 us; the launch traced here: 36.5 us
  Pallas kernels  34.9 us (95%)
  local copies, waits for them, and re-layouts  1.67 us (5%)
    pallas_call x1, Pallas kernels, local(): pl.pallas_call(kernel, out_shape=jax.ShapeDtypeStruct((sources // 4, rows...  34.9 us
    unnamed x1, local copies, waits for them, and re-layouts  1.67 us

profile of v6, /device:TPU:0, one launch (start us, length us, event | category | flops | bytes accessed | tf_op | source)
XLA Modules:
  0.0 36.5 jit_solution(216490927649464111)
XLA Ops:
  0.0 34.9 %shard_map.73 = f32[2,32,1024]{2,1,0:T(8,128)} custom-call(bf16[4,8,32,1024]{3,2,1,0:T(8,128)(2,1)} %fields_in.1, f32[32,1024]{1,0:T(8,128)} %sigma_in.1, f32[16]{0:T(128)} %wavenumbers_in.1, f32[16]{0:T(128)} %weights_in.1, s32[16]{0:T(128)} %counts_in.1, s32[64]{0:T(128)} %electrodes_in.1, s32[2,8]{1,0:T(2,128)} %bitcast.1), custom_call_target="tpu_custom_call" | custom-call | tf_op jit(solution)/shard_map/pallas_call | solution.py:371
  34.9 1.7 %copy.9 = f32[2,32,1024]{2,1,0:T(8,128)} copy(f32[2,32,1024]{2,1,0:T(8,128)} %shard_map.73) | data formatting | bytes 524288

commit v7 on v6

--- a/solution.py
+++ b/solution.py
@@ -28,7 +28,8 @@
 FIRST = 8
 CORE = FIRST + HALO
 LAST = FIRST + HELD
-UNROLL = ((8, 6), (9, 5), (11, 4), (7, 6), (8, 5), (8, 5), (7, 5), (11, 3))
+UNROLL = ((8, 6), (9, 5), (11, 4), (7, 6), (13, 3), (19, 2), (7, 5), (11, 3))
+FIRST_TWINS = 11
 MESH = pl.DeviceIdType.MESH
 F32 = jnp.float32
 BF16 = jnp.bfloat16
@@ -237,26 +238,34 @@
 
     lax.fori_loop(0, HELD // 4, four_rows, (zero,) * PARTS)
 
-    def sweep(step):
+    def sweep(step, pair, spots):
         now, later = step % 2, (step + 1) % 2
-        before = now if step == 0 else later
         charge = vectors[3 * step + 2, pl.ds(0, SUBS), :]
         start = FIRST + step + 1
         unroll, blocks = UNROLL[step]
         parts = [pl.ds(part * SUBS, SUBS) for part in range(PARTS)]
 
-        def one(row, carry):
+        def one(row, carry, u):
             old, sums = carry
-            edge = pltpu.roll(w[now, row, parts[-1], :], 1, 1)
-            u, held, flow_first = [], [], None
+            edge = pltpu.roll(u[-1], 1, 1)
+            held, flow_first = [], None
+            if step == 0:
+                spot = jnp.where(row - 1 == spots[0], CURRENT, 0.0) - jnp.where(row - 1 == spots[1], CURRENT, 0.0)
+                source = jnp.where(first_lane, (2.0 / DELTA) * spot * src[1, row - 1], 0.0)
+                src[0, row - 1] = source
+            else:
+                source = src[0, row - 1]
             for part, at in enumerate(parts):
-                here = w[now, row, at, :]
+                here = u[part]
                 north_c = an[row, at, :]
                 side_gain, centre_gain = vectors[3 * step + 1, at, :], vectors[3 * step, at, :]
-                value = side_gain * (sums[part] + north_c * here) + (
-                    centre_gain * old[part] - w[before, row - 1, at, :])
+                if step == 0:
+                    value = side_gain * (sums[part] + north_c * here) + (centre_gain - 1.0) * old[part]
+                else:
+                    value = side_gain * (sums[part] + north_c * here) + (
+                        centre_gain * old[part] - w[later, row - 1, at, :])
                 if part == 0:
-                    value = value + charge * src[0, row - 1]
+                    value = value + charge * source
                 w[later, row - 1, at, :] = value
                 west_c = aw[row, at, :]
                 flow = west_c * here
@@ -264,18 +273,48 @@
                     flow_first = pltpu.roll(flow, LANES - 1, 1)
                 else:
                     held[-1] = held[-1] + flow
-                held.append(north_c * old[part] + west_c * (u[-1] if part else edge))
-                u.append(here)
+                held.append(north_c * old[part] + west_c * (u[part - 1] if part else edge))
             held[-1] = held[-1] + flow_first
             return tuple(u), tuple(held)
 
-        def body(block, carry):
-            for place in range(unroll):
-                carry = one(start + unroll * block + place, carry)
+        def given(twin):
+            both = [[], []]
+            for part, at in enumerate(parts):
+                values = stage[pair, pl.ds(twin * 2 * SUBS, 2 * SUBS), pl.ds(part * LANES, LANES)].astype(F32)
+                for place in range(2):
+                    row = FIRST + 2 * twin + place
+                    value = values[place * SUBS:(place + 1) * SUBS] * root[row, at, :]
+                    w[0, row, at, :] = value
+                    both[place].append(value)
+            return both
+
+        def two(twin, carry):
+            row = FIRST + 2 * twin
+            for place, u in enumerate(given(twin)):
+                carry = one(row + place, carry, u)
             return carry
 
-        opening = tuple(w[now, start - 1, at, :] for at in parts)
-        lax.fori_loop(0, blocks, body, (opening, (zero,) * PARTS))
+        if step == 0:
+            opening, second = given(0)
+            carry = one(FIRST + 1, (tuple(opening), (zero,) * PARTS), second)
+            carry = two(1, carry)
+
+            def several(block, carry):
+                for place in range(FIRST_TWINS):
+                    carry = two(2 + FIRST_TWINS * block + place, carry)
+                return carry
+
+            lax.fori_loop(0, (HELD // 2 - 2) // FIRST_TWINS, several, carry)
+        else:
+
+            def body(block, carry):
+                for place in range(unroll):
+                    row = start + unroll * block + place
+                    carry = one(row, carry, [w[now, row, at, :] for at in parts])
+                return carry
+
+            opening = tuple(w[now, start - 1, at, :] for at in parts)
+            lax.fori_loop(0, blocks, body, (opening, (zero,) * PARTS))
 
     def rs_copies(pair):
         slot = 2 * pair
@@ -294,23 +333,8 @@
         for copy in halo_copies(pair):
             copy.wait_recv()
 
-        @pl.loop(0, HELD // 4)
-        def _(block):
-            for twin in (2 * block, 2 * block + 1):
-                for part in range(PARTS):
-                    rows8 = pl.ds(part * SUBS, SUBS)
-                    given = stage[pair, pl.ds(twin * 2 * SUBS, 2 * SUBS), pl.ds(part * LANES, LANES)].astype(F32)
-                    for place in range(2):
-                        row = FIRST + 2 * twin + place
-                        w[0, row, rows8, :] = given[place * SUBS:(place + 1) * SUBS] * root[row, rows8, :]
-            for place in range(4):
-                row = FIRST + 4 * block + place
-                spot = jnp.where(row == spots[0], CURRENT, 0.0) - jnp.where(row == spots[1], CURRENT, 0.0)
-                spot = (2.0 / DELTA) * spot * src[1, row]
-                src[0, row] = jnp.where(first_lane, spot, 0.0)
-
         for step in range(ITERS):
-            sweep(step)
+            sweep(step, pair, spots)
 
         @pl.loop(0, ROWS // 4)
         def _(block):

time: 36.7 us -> 36.3 us (0.989)
  Pallas kernels: 34.9 us -> 34.5 us
    pallas_call x1, Pallas kernels: 34.9 us -> 34.5 us  [local(): pl.pallas_call(kernel, out_shape=jax.ShapeDtypeStruct((sources // 4, rows...]
where the time goes in v7:
time: 36.3 us; the launch traced here: 36.1 us
  Pallas kernels  34.5 us (95%)
  local copies, waits for them, and re-layouts  1.67 us (5%)
    pallas_call x1, Pallas kernels, local(): pl.pallas_call(kernel, out_shape=jax.ShapeDtypeStruct((sources // 4, rows...  34.5 us
    unnamed x1, local copies, waits for them, and re-layouts  1.67 us

profile of v7, /device:TPU:0, one launch (start us, length us, event | category | flops | bytes accessed | tf_op | source)
XLA Modules:
  0.0 36.1 jit_solution(12747378015642258260)
XLA Ops:
  0.0 34.5 %shard_map.73 = f32[2,32,1024]{2,1,0:T(8,128)} custom-call(bf16[4,8,32,1024]{3,2,1,0:T(8,128)(2,1)} %fields_in.1, f32[32,1024]{1,0:T(8,128)} %sigma_in.1, f32[16]{0:T(128)} %wavenumbers_in.1, f32[16]{0:T(128)} %weights_in.1, s32[16]{0:T(128)} %counts_in.1, s32[64]{0:T(128)} %electrodes_in.1, s32[2,8]{1,0:T(2,128)} %bitcast.1), custom_call_target="tpu_custom_call" | custom-call | tf_op jit(solution)/shard_map/pallas_call | solution.py:395
  34.5 1.7 %copy.9 = f32[2,32,1024]{2,1,0:T(8,128)} copy(f32[2,32,1024]{2,1,0:T(8,128)} %shard_map.73) | data formatting | bytes 524288

commit v8 on v7

--- a/solution.py
+++ b/solution.py
@@ -28,7 +28,7 @@
 FIRST = 8
 CORE = FIRST + HALO
 LAST = FIRST + HELD
-UNROLL = ((8, 6), (9, 5), (11, 4), (7, 6), (13, 3), (19, 2), (7, 5), (11, 3))
+UNROLL = ((8, 6), (15, 3), (22, 2), (21, 2), (13, 3), (19, 2), (18, 2), (17, 2))
 FIRST_TWINS = 11
 MESH = pl.DeviceIdType.MESH
 F32 = jnp.float32
@@ -336,9 +336,9 @@
         for step in range(ITERS):
             sweep(step, pair, spots)
 
-        @pl.loop(0, ROWS // 4)
+        @pl.loop(0, ROWS // 8)
         def _(block):
-            for row in [4 * block + place for place in range(4)]:
+            for row in [8 * block + place for place in range(8)]:
                 for part in range(PARTS):
                     rows8 = pl.ds(part * SUBS, SUBS)
                     value = close[CORE + row, rows8, :] * w[ITERS % 2, CORE + row, rows8, :]

time: 36.3 us -> 35.9 us (0.989)
  Pallas kernels: 34.5 us -> 34.1 us
where the time goes in v8:
time: 35.9 us; the launch traced here: 35.8 us
  Pallas kernels  34.1 us (95%)
  local copies, waits for them, and re-layouts  1.67 us (5%)
    pallas_call x1, Pallas kernels, local(): pl.pallas_call(kernel, out_shape=jax.ShapeDtypeStruct((sources // 4, rows...  34.1 us
    unnamed x1, local copies, waits for them, and re-layouts  1.67 us

profile of v8, /device:TPU:0, one launch (start us, length us, event | category | flops | bytes accessed | tf_op | source)
XLA Modules:
  0.0 35.8 jit_solution(1013711947201313685)
XLA Ops:
  0.0 34.1 %shard_map.73 = f32[2,32,1024]{2,1,0:T(8,128)} custom-call(bf16[4,8,32,1024]{3,2,1,0:T(8,128)(2,1)} %fields_in.1, f32[32,1024]{1,0:T(8,128)} %sigma_in.1, f32[16]{0:T(128)} %wavenumbers_in.1, f32[16]{0:T(128)} %weights_in.1, s32[16]{0:T(128)} %counts_in.1, s32[64]{0:T(128)} %electrodes_in.1, s32[2,8]{1,0:T(2,128)} %bitcast.1), custom_call_target="tpu_custom_call" | custom-call | tf_op jit(solution)/shard_map/pallas_call | solution.py:395
  34.1 1.7 %copy.9 = f32[2,32,1024]{2,1,0:T(8,128)} copy(f32[2,32,1024]{2,1,0:T(8,128)} %shard_map.73) | data formatting | bytes 524288

commit v9 on v8

--- a/solution.py
+++ b/solution.py
@@ -142,19 +142,22 @@
                    h_send.at[1, pair], h_recv.at[1, pair], north),
         )
 
-    @pl.loop(0, 2)
-    def _(batch):
+    def gather(batch, extra):
         woven = []
         for pair in (2 * batch, 2 * batch + 1):
             columns = [slot_column(pair, half, wave_pos) for half in range(2)]
             block = jnp.concatenate(
                 [fields[k, columns[half]] for half in range(2) for k in range(per_group)], axis=0)
             woven.append(jnp.dot(weave[...], block, preferred_element_type=F32).astype(BF16))
-        moved = jnp.dot(jnp.concatenate(woven, axis=0), into[...], preferred_element_type=F32).astype(BF16)
+        moved = jnp.dot(jnp.concatenate(woven + extra, axis=0), into[...], preferred_element_type=F32)
         for place, pair in enumerate((2 * batch, 2 * batch + 1)):
-            stage[pair, pl.ds(HALO * SUBS, ROWS * SUBS), :] = moved[place * ROWS * SUBS:(place + 1) * ROWS * SUBS]
+            stage[pair, pl.ds(HALO * SUBS, ROWS * SUBS), :] = moved[
+                place * ROWS * SUBS:(place + 1) * ROWS * SUBS].astype(BF16)
             for copy in halo_copies(pair):
                 copy.start()
+        return moved[2 * ROWS * SUBS:]
+
+    gather(0, [])
 
     def by_wavenumber(scalars):
         value = zero
@@ -180,7 +183,7 @@
     sig_south.wait_recv()
     sig_north.wait_recv()
     whole = jnp.concatenate([sig_n[...], sigma[...], sig_s[...]], axis=0)
-    moved = jnp.dot(jnp.concatenate(thirds(whole), axis=0), into[...], preferred_element_type=F32)
+    moved = gather(1, list(thirds(whole)))
     moved = (moved[:HELD] + moved[HELD:2 * HELD]) + moved[2 * HELD:]
     for part in range(PARTS):
         sig[part, pl.ds(FIRST, HELD), :] = moved[:, part * LANES:(part + 1) * LANES]

time: 35.9 us -> 36.9 us (1.028)
  Pallas kernels: 34.1 us -> 35.1 us
    pallas_call x1, Pallas kernels: 34.1 us -> 35.1 us  [local(): pl.pallas_call(kernel, out_shape=jax.ShapeDtypeStruct((sources // 4, rows...]
where the time goes in v9:
time: 36.9 us; the launch traced here: 36.8 us
  Pallas kernels  35.1 us (95%)
  local copies, waits for them, and re-layouts  1.67 us (5%)
    pallas_call x1, Pallas kernels, local(): pl.pallas_call(kernel, out_shape=jax.ShapeDtypeStruct((sources // 4, rows...  35.1 us
    unnamed x1, local copies, waits for them, and re-layouts  1.67 us

profile of v9, /device:TPU:0, one launch (start us, length us, event | category | flops | bytes accessed | tf_op | source)
XLA Modules:
  0.0 36.8 jit_solution(12447840991252227776)
XLA Ops:
  0.0 35.1 %shard_map.73 = f32[2,32,1024]{2,1,0:T(8,128)} custom-call(bf16[4,8,32,1024]{3,2,1,0:T(8,128)(2,1)} %fields_in.1, f32[32,1024]{1,0:T(8,128)} %sigma_in.1, f32[16]{0:T(128)} %wavenumbers_in.1, f32[16]{0:T(128)} %weights_in.1, s32[16]{0:T(128)} %counts_in.1, s32[64]{0:T(128)} %electrodes_in.1, s32[2,8]{1,0:T(2,128)} %bitcast.1), custom_call_target="tpu_custom_call" | custom-call | tf_op jit(solution)/shard_map/pallas_call | solution.py:398
  35.1 1.7 %copy.9 = f32[2,32,1024]{2,1,0:T(8,128)} copy(f32[2,32,1024]{2,1,0:T(8,128)} %shard_map.73) | data formatting | bytes 524288
